TPU v7x, 32 devices: a whole 2x2x4 slice. The times are simulated.
32 devices in a mesh: ctx: 8 (over z, x), zero: 4 (over y, core).
Axes of the slice: x: 2, y: 2, z: 4, core: 2. Of those that a mesh axis runs over, the one named last changes fastest.
Arguments:
- activations: bfloat16 [4096, 4096], P('ctx', 'zero'), may hold values from -1200 to 1200
- norm_gain: bfloat16 [4096], replicated, may hold values from 0.099609375 to 1.8984375
- query_weight: bfloat16 [4096, 1024], P('ctx', 'zero'), may hold values from -24 to 24
- kv_weight: bfloat16 [4096, 4, 128], P('ctx', 'zero'), may hold values from -1 to 1
- out_weight: bfloat16 [1024, 4096], P('zero', 'ctx'), may hold values from -0.1875 to 0.1875
- tile_mask: int32 [8, 4, 4], P('ctx'), may hold values from 0 to 1, as said below
- anchor_mask: int32 [8, 4, 4], P('ctx'), may hold values 0 or 1
- anchor_index: int32 [1], replicated, may hold values from 0 to 7
Outputs:
- mixed: bfloat16 [4096, 4096], P(('ctx', 'zero'))
Inputs may be any that keep to these rules, and one draw needn't show every extreme that they name: `tile_mask`: entries of every block's table above the diagonal are 0 and diagonal entries are 1.
All inputs are finite; a program needn't handle non-finite values. No bound on the sum of `anchor_mask` on one device may be relied on, other than what follows from the above.
Results may differ from a plain program's by a relative error of at most 0.02.
Values may be sent and summed in bfloat16 or wider, within the bound.
No kernel may reach another device: no remote copies, remote signals or barrier semaphores. Data moves between devices by JAX's collectives and lax.ppermute only.
A program may use at most 64 MiB of HBM per device.

v0:
```python
import functools
import math

import jax
import jax.numpy as jnp
from jax import lax
from jax.experimental import pallas as pl
from jax.experimental.pallas import tpu as pltpu
from jax.sharding import PartitionSpec as P

HBM = pl.BlockSpec(memory_space=pltpu.HBM)
VMEM = pl.BlockSpec(memory_space=pltpu.VMEM)
SMEM = pl.BlockSpec(memory_space=pltpu.SMEM)
VMEM_LIMIT = 48 * 1024 * 1024
ROPE_BASE = 500000.0
CHUNKS = 4


def swap(value, axis, stride):
    pairs = [(source, source ^ stride) for source in range(lax.axis_size(axis))]
    return lax.ppermute(value, axis, pairs)


def cycle(size):
    return list(range(0, size, 2)) + list(range(1, size, 2))[::-1]


def ring_step(value):
    ctx_size, zero_size = lax.axis_size("ctx"), lax.axis_size("zero")
    order = cycle(ctx_size)
    pairs = []
    for at in range(ctx_size):
        for zero in range(zero_size):
            to = order[(at + (1 if zero % 2 == 0 else -1)) % ctx_size]
            pairs.append((order[at] * zero_size + zero, to * zero_size + zero))
    return lax.ppermute(value, ("ctx", "zero"), pairs)


def ring_gather(shard, core):
    size = lax.axis_size("ctx")
    held = [(0, None, shard)]
    moving = shard
    half = shard.shape[0] // 2
    for step in range(1, size // 2 + 1):
        last = step == size // 2
        if last:
            moving = lax.dynamic_slice_in_dim(moving, core * half, half, 0)
        moving = ring_step(moving)
        held.append((-step, 0 if last else None, moving))
        held.append((step, 1 if last else None, swap(moving, "zero", 1)))
    return held


def source_of(steps):
    size = lax.axis_size("ctx")
    ctx, core = lax.axis_index("ctx"), lax.axis_index("zero") % 2
    place = jnp.where(ctx % 2 == 0, ctx // 2, size - 1 - ctx // 2)
    place = lax.rem(place + steps * (1 - 2 * core) + size, size)
    return jnp.where(place < size // 2, 2 * place, 2 * (size - 1 - place) + 1)


def share_of(share):
    core = lax.axis_index("zero") % 2
    return core if share == 0 else 1 - core


def project_kernel(layout, pieces, first_call, *refs):
    (x_buf, w_buf, x_sem, w_sem) = refs[-4:]
    scale_ref, cos_ref, sin_ref = refs[:3]
    x_refs = refs[3 : 3 + pieces]
    w_refs = refs[3 + pieces : 3 + pieces + len(layout)]
    out_ref = refs[3 + pieces + len(layout)]
    zero = lax.axis_index("zero")
    shard_rows = w_refs[0].shape[0]
    x_copies, w_copies = [], []
    for at, ref in enumerate(x_refs):
        place = jnp.bitwise_xor(zero, at)
        x_copies.append(pltpu.make_async_copy(ref, x_buf.at[place], x_sem.at[at]))
    for at, (ref, (steps, share)) in enumerate(zip(w_refs, layout)):
        start = source_of(steps) * shard_rows
        if share is not None:
            start = start + share_of(share) * ref.shape[0]
        rows = pl.ds(pl.multiple_of(start, 16), ref.shape[0])
        w_copies.append(pltpu.make_async_copy(ref, w_buf.at[rows], w_sem.at[at]))
    for copy in x_copies + w_copies:
        copy.start()
    for copy in x_copies:
        copy.wait()
    depth = x_buf.shape[2]
    if first_call:
        squares = jnp.zeros((x_buf.shape[1], 128), jnp.float32)
        for at in range(pieces):
            for first in range(0, depth, 128):
                x_float = x_buf[at, :, first : first + 128].astype(jnp.float32)
                squares += x_float * x_float
        mean = jnp.sum(squares, axis=1, keepdims=True) / (depth * pieces)
        scale = jnp.broadcast_to(lax.rsqrt(mean + 1e-05), squares.shape)
        scale_out = refs[4 + pieces + len(layout)]
        scale_out[...] = scale
    else:
        scale = scale_ref[...]
    for copy in w_copies:
        copy.wait()
    total = jnp.zeros(out_ref.shape, jnp.float32)
    for at in range(pieces):
        total += jnp.dot(
            x_buf[at], w_buf[at * depth : (at + 1) * depth, :], preferred_element_type=jnp.float32
        )
    head = cos_ref.shape[1]
    for first in range(0, out_ref.shape[1], head):
        part = total[:, first : first + head] * scale
        if not first_call or first == 0:
            part = part * cos_ref[...] + pltpu.roll(part, head // 2, 1) * sin_ref[...]
        out_ref[:, first : first + head] = part.astype(out_ref.dtype)


def project(scale, cos, sin, x_pieces, held, first_call):
    layout = [(steps, share) for steps, share, _ in held]
    shards = [piece for _, _, piece in held]
    tokens, depth = x_pieces[0].shape
    width = shards[0].shape[1]
    full = depth * len(x_pieces)
    out = [jax.ShapeDtypeStruct((tokens, width), jnp.bfloat16)]
    if first_call:
        out.append(jax.ShapeDtypeStruct((tokens, 128), jnp.float32))
    return pl.pallas_call(
        functools.partial(project_kernel, layout, len(x_pieces), first_call),
        out_shape=out,
        in_specs=[VMEM, VMEM, VMEM] + [HBM] * (len(x_pieces) + len(shards)),
        out_specs=[VMEM] * len(out),
        scratch_shapes=[
            pltpu.VMEM((len(x_pieces), tokens, depth), jnp.bfloat16),
            pltpu.VMEM((full, width), jnp.bfloat16),
            pltpu.SemaphoreType.DMA((len(x_pieces),)),
            pltpu.SemaphoreType.DMA((len(shards),)),
        ],
        compiler_params=pltpu.CompilerParams(vmem_limit_bytes=VMEM_LIMIT),
        cost_estimate=pl.CostEstimate(
            flops=2 * tokens * full * width,
            bytes_accessed=2 * full * (tokens + width),
            transcendentals=0,
        ),
    )(scale, cos, sin, *x_pieces, *shards)


def attend_kernel(groups, own_ref, far_ref, q_ref, near0, near1, far0, far1, out_ref):
    tokens, pair = near0.shape
    head = pair // 2
    size = tokens // groups
    tiles = own_ref.shape[0]
    tile = 2 * tokens // tiles
    heads = q_ref.shape[1] // head
    rows = heads * size
    core = lax.axis_index("zero") % 2
    column = lax.broadcasted_iota(jnp.int32, (1, tokens), 1)
    column_group = column // size
    within = lax.rem(lax.broadcasted_iota(jnp.int32, (rows, 1), 0), size)
    hidden = jnp.float32(-1e30)
    nt = (((1,), (1,)), ((), ()))
    for h in range(groups):
        across = slice(h * size, (h + 1) * size)
        q = jnp.concatenate(
            [q_ref[across, g * head : (g + 1) * head] for g in range(heads)], axis=0
        )
        first = (2 * h + core) * size
        own_tile = first // tile
        seen = min(tokens, -(-(h + 1) * size // 128) * 128)
        parts, blocks = [], []
        for ref, mask_ref, width, parity, causal in (
            (far0, far_ref, tokens, core, False),
            (far1, far_ref, tokens, 1 - core, False),
            (near0, own_ref, seen, core, True),
            (near1, own_ref, seen, 1 - core, True),
        ):
            visible = jnp.zeros((1, width), jnp.int32)
            for g in range(-(-width // size)):
                at = mask_ref[own_tile, (2 * g + parity) * size // tile]
                visible = jnp.where(column_group[:, :width] == g, at, visible)
            visible = visible == 1
            if causal:
                group = column_group[:, :width]
                offset = (2 * group + parity) * size + column[:, :width] - group * size
                visible = visible & (offset <= first + within)
            scores = lax.dot_general(
                q, ref[:width, :head], nt, preferred_element_type=jnp.float32
            )
            parts.append(jnp.where(visible, scores, hidden))
            blocks.append((ref, width))
        scores = jnp.concatenate(parts, axis=1)
        largest = jnp.max(scores, axis=1, keepdims=True)
        weights = jnp.exp(scores - largest)
        total = jnp.sum(weights, axis=1, keepdims=True)
        rounded = weights.astype(jnp.bfloat16)
        mixed = jnp.zeros((rows, head), jnp.float32)
        start = 0
        for ref, width in blocks:
            mixed += jnp.dot(
                rounded[:, start : start + width],
                ref[:width, head:],
                preferred_element_type=jnp.float32,
            )
            start += width
        mixed = (mixed / total).astype(out_ref.dtype)
        for g in range(heads):
            out_ref[across, g * head : (g + 1) * head] = mixed[g * size : (g + 1) * size, :]


def attend(groups, own_mask, far_mask, queries, near, near_other, far, far_other):
    tokens, width = queries.shape
    return pl.pallas_call(
        functools.partial(attend_kernel, groups),
        out_shape=jax.ShapeDtypeStruct(queries.shape, jnp.bfloat16),
        in_specs=[SMEM, SMEM] + [VMEM] * 5,
        out_specs=VMEM,
        compiler_params=pltpu.CompilerParams(vmem_limit_bytes=VMEM_LIMIT),
        cost_estimate=pl.CostEstimate(
            flops=16 * tokens * tokens * width,
            bytes_accessed=8 * tokens * width,
            transcendentals=16 * tokens * tokens,
        ),
    )(own_mask, far_mask, queries, near, near_other, far, far_other)


def terms_kernel(layout, split, a_ref, *refs):
    keep_ref, send_ref, w_buf, sem = refs[-4:]
    half = keep_ref.shape[0]
    width = w_buf.shape[2]
    copies = []
    for at, (ref, (slot, share)) in enumerate(zip(refs[:-4], layout)):
        target = w_buf.at[slot]
        if share is not None:
            rows = ref.shape[0]
            target = w_buf.at[slot, pl.ds(pl.multiple_of(share_of(share) * rows, 16), rows)]
        copies.append(pltpu.make_async_copy(ref, target, sem.at[at]))
    for copy in copies:
        copy.start()
    pick = lax.axis_index("zero") // split % 2
    mine = a_ref[pl.ds(pl.multiple_of(pick * half, 16), half), :]
    other = a_ref[pl.ds(pl.multiple_of((1 - pick) * half, 16), half), :]
    both = jnp.concatenate([other, mine], axis=0)
    for copy in copies:
        copy.wait()
    for slot in range(w_buf.shape[0]):
        out = jnp.dot(both, w_buf[slot], preferred_element_type=jnp.float32)
        columns = slice(slot * width, (slot + 1) * width)
        send_ref[:, columns] = out[:half].astype(send_ref.dtype)
        keep_ref[:, columns] = out[half:]


def terms(split, attended, slots):
    layout = [(slot, share) for slot, pieces in enumerate(slots) for share, _ in pieces]
    shards = [piece for pieces in slots for _, piece in pieces]
    width = shards[0].shape[1]
    rows, depth = attended.shape
    columns = width * len(slots)
    return pl.pallas_call(
        functools.partial(terms_kernel, layout, split),
        out_shape=(
            jax.ShapeDtypeStruct((rows // 2, columns), jnp.float32),
            jax.ShapeDtypeStruct((rows // 2, columns), jnp.bfloat16),
        ),
        in_specs=[VMEM] + [HBM] * len(shards),
        out_specs=(VMEM, VMEM),
        scratch_shapes=[
            pltpu.VMEM((len(slots), depth, width), jnp.bfloat16),
            pltpu.SemaphoreType.DMA((len(shards),)),
        ],
        compiler_params=pltpu.CompilerParams(vmem_limit_bytes=VMEM_LIMIT),
        cost_estimate=pl.CostEstimate(
            flops=2 * rows * depth * columns,
            bytes_accessed=2 * (rows + columns) * depth + 3 * rows * columns,
            transcendentals=0,
        ),
    )(attended, *shards)


def join_kernel(groups, *refs):
    out_ref = refs[-1]
    count = len(groups)
    width = out_ref.shape[1] // sum(len(group) for group in groups)
    for group, keep_ref, got_ref in zip(groups, refs[:count], refs[count:-1]):
        for slot, steps in enumerate(group):
            columns = slice(slot * width, (slot + 1) * width)
            start = pl.multiple_of(source_of(steps) * width, 128)
            total = keep_ref[:, columns] + got_ref[:, columns].astype(jnp.float32)
            out_ref[:, pl.ds(start, width)] = total.astype(out_ref.dtype)


def join(groups, keeps, gots):
    rows = keeps[0].shape[0]
    columns = sum(keep.shape[1] for keep in keeps)
    return pl.pallas_call(
        functools.partial(join_kernel, groups),
        out_shape=jax.ShapeDtypeStruct((rows, columns), jnp.bfloat16),
        in_specs=[VMEM] * (2 * len(keeps)),
        out_specs=VMEM,
        compiler_params=pltpu.CompilerParams(vmem_limit_bytes=VMEM_LIMIT),
        cost_estimate=pl.CostEstimate(
            flops=rows * columns, bytes_accessed=8 * rows * columns, transcendentals=0
        ),
    )(*keeps, *gots)


def broadcast_from(value, root):
    me = lax.axis_index("ctx")
    for bit in range(int(math.log2(lax.axis_size("ctx")))):
        other = swap(value, "ctx", 1 << bit)
        same = ((me >> bit) & 1) == ((root >> bit) & 1)
        value = jnp.where(same, value, other)
    return value


def local(
    activations,
    norm_gain,
    query_weight,
    kv_weight,
    out_weight,
    tile_mask,
    anchor_mask,
    anchor_index,
):
    tokens, depth = activations.shape
    head = kv_weight.shape[2]
    ctx_size, zero_size = lax.axis_size("ctx"), lax.axis_size("zero")
    ctx_rank, zero_rank = lax.axis_index("ctx"), lax.axis_index("zero")
    core = zero_rank % 2
    groups = zero_size // 2
    size = tokens // zero_size

    by_core = activations.reshape(groups, 2, size, depth)
    mine = lax.dynamic_index_in_dim(by_core, core, 1, keepdims=False).reshape(-1, depth)
    theirs = lax.dynamic_index_in_dim(by_core, 1 - core, 1, keepdims=False).reshape(-1, depth)
    x_pieces = [mine] + [
        swap(theirs if m % 2 else mine, "zero", m) for m in range(1, zero_size)
    ]

    shard_rows = kv_weight.shape[0]
    gain = lax.dynamic_slice_in_dim(norm_gain, ctx_rank * shard_rows, shard_rows)
    gain = gain.astype(jnp.float32)[:, None]

    def of_chip(own, axis):
        other = swap(own, "zero", 1)
        return jnp.where(
            core == 0,
            jnp.concatenate([own, other], axis),
            jnp.concatenate([other, own], axis),
        )

    kv_pair = (of_chip(kv_weight[:, 0, :], 1).astype(jnp.float32) * gain).astype(jnp.bfloat16)
    query_pair = (of_chip(query_weight, 1).astype(jnp.float32) * gain).astype(jnp.bfloat16)
    out_pair = of_chip(out_weight, 0)
    kv_held = ring_gather(kv_pair, core)
    query_held = ring_gather(query_pair, core)
    out_held = ring_gather(out_pair, core)

    half = head // 2
    frequency = jnp.power(
        jnp.float32(ROPE_BASE), -(jnp.arange(half, dtype=jnp.float32) * 2.0 / head)
    )
    local_token = jnp.arange(tokens // 2, dtype=jnp.int32)
    offsets = (2 * (local_token // size) + core) * size + local_token % size
    positions = ctx_rank * tokens + offsets
    angles = positions.astype(jnp.float32)[:, None] * frequency[None, :]
    cos_half, sin_half = jnp.cos(angles), jnp.sin(angles)
    cos = jnp.concatenate([cos_half, cos_half], -1)
    sin = jnp.concatenate([-sin_half, sin_half], -1)
    shrink = head ** (-0.5)

    near, scale = project(cos, cos, sin, x_pieces, kv_held, True)
    anchor = anchor_index[0]
    far = broadcast_from(near, anchor)
    near_other = swap(near, "zero", 1)
    far_other = swap(far, "zero", 1)
    (queries,) = project(scale, cos * shrink, sin * shrink, x_pieces, query_held, False)
    far_mask = jnp.where(ctx_rank != anchor, anchor_mask[0], 0)
    attended = attend(groups, tile_mask[0], far_mask, queries, near, near_other, far, far_other)

    slots = []
    for steps, share, piece in out_held:
        if share == 1:
            slots[-1][1].append((share, piece))
        else:
            slots.append((steps, [(share, piece)]))
    per = max(1, ctx_size // CHUNKS)
    step_groups, keeps, gots = [], [], []
    top = zero_size // 2
    for at in range(0, ctx_size, per):
        step_groups.append([steps for steps, _ in slots[at : at + per]])
        keep, send = terms(top, attended, [pieces for _, pieces in slots[at : at + per]])
        got = swap(send, "zero", top)
        stride = top // 2
        while stride > 1:
            both = keep + got.astype(jnp.float32)
            rows = both.shape[0] // 2
            bit = (zero_rank // stride) % 2
            keep = lax.dynamic_slice_in_dim(both, bit * rows, rows, 0)
            send = lax.dynamic_slice_in_dim(both, (1 - bit) * rows, rows, 0)
            got = swap(send.astype(jnp.bfloat16), "zero", stride)
            stride //= 2
        keeps.append(keep)
        gots.append(got)
    return join(step_groups, keeps, gots)


def solution(mesh):
    placed = (
        P("ctx", "zero"),
        P(),
        P("ctx", "zero"),
        P("ctx", "zero", None),
        P("zero", "ctx"),
        P("ctx", None, None),
        P("ctx", None, None),
        P(),
    )
    return jax.shard_map(
        local, mesh=mesh, in_specs=placed, out_specs=P(("ctx", "zero"), None), check_vma=False
    )
```

profile of v0, /device:TPU:0, one launch (start us, length us, event | category | flops | bytes accessed | tf_op | source)
XLA Modules:
  0.0 119.4 jit_solution(11833403484878105715)
XLA Ops:
  1.0 0.8 dynamic-slice_convert_fusion
  1.7 1.1 multiply_convert_fusion.1.refs_7_
  2.8 2.9 %collective-permute-start.4 = (bf16[512,256]{1,0:T(8,128)(2,1)S(1)}, bf16[512,256]{1,0:T(8,128)(2,1)S(1)}, u32[]{:S(2)}, u32[]{:S(2)}) collective-permute-start(bf16[512,256]{1,0:T(8,128)(2,1)S(1)} %multiply_convert_fusion.1.refs_7_), channel_id=1, source_target_pairs={{0,8},{1,5},{2,10},{3,7},{8,16},{9,1},{10,18},{11,3},{16,24},{17,9... | collective-permute-start | bytes 786440 | tf_op jit(solution)/shard_map/ppermute | solution.py:36
  5.8 2.1 %constant_dynamic-slice_fusion.3 = (bf16[2,1,128,1024]{3,2,1,0:T(8,128)(2,1)}, bf16[2,1,128,1024]{3,2,1,0:T(8,128)(2,1)S(1)}) fusion(bf16[2,2,128,1024]{3,2,1,0:T(8,128)(2,1)} %bitcast.20, s32[]{:T(128)S(6)} %select_n.98, s32[]{:T(128)S(6)} %select_n.97), kind=kLoop, calls=%fused_computation.26 | loop fusion | bytes 2097160 | tf_op jit(solution)/shard_map/jit(dynamic_index_in_dim)/dynamic_slice | solution.py:333
  8.1 1.6 %collective-permute-start.13 = (bf16[512,512]{1,0:T(8,128)(2,1)S(1)}, bf16[512,512]{1,0:T(8,128)(2,1)}, u32[]{:S(2)}, u32[]{:S(2)}) collective-permute-start(bf16[512,512]{1,0:T(8,128)(2,1)S(1)} %multiply_convert_fusion.refs_7_), channel_id=1, source_target_pairs={{0,8},{1,5},{2,10},{3,7},{8,16},{9,1},{10,18},{11,3},{16,24},{17,9... | collective-permute-start | bytes 1572872 | tf_op jit(solution)/shard_map/ppermute | solution.py:36
  10.0 2.1 %collective-permute-start.6 = (bf16[512,256]{1,0:T(8,128)(2,1)S(1)}, bf16[512,256]{1,0:T(8,128)(2,1)}, u32[]{:S(2)}, u32[]{:S(2)}) collective-permute-start(bf16[512,256]{1,0:T(8,128)(2,1)S(1)} %collective-permute-done.4.refs_8_), channel_id=1, source_target_pairs={{0,8},{1,5},{2,10},{3,7},{8,16},{9,1},{10,18},{11,3},{16,24},{17,9... | collective-permute-start | bytes 786440 | tf_op jit(solution)/shard_map/ppermute | solution.py:36
  12.4 1.6 %collective-permute-start.27 = (bf16[512,512]{1,0:T(8,128)(2,1)S(1)}, bf16[512,512]{1,0:T(8,128)(2,1)}, u32[]{:S(2)}, u32[]{:S(2)}) collective-permute-start(bf16[512,512]{1,0:T(8,128)(2,1)S(1)} %maximum_select_fusion.1.refs_0_), channel_id=1, source_target_pairs={{0,8},{1,5},{2,10},{3,7},{8,16},{9,1},{10,18},{11,3},{16,24},{17,9... | collective-permute-start | bytes 1572872 | tf_op jit(solution)/shard_map/ppermute | solution.py:36
  14.0 1.5 %collective-permute-start.1 = (bf16[256,1024]{1,0:T(8,128)(2,1)S(1)}, bf16[256,1024]{1,0:T(8,128)(2,1)S(1)}, u32[]{:S(2)}, u32[]{:S(2)}) collective-permute-start(bf16[256,1024]{1,0:T(8,128)(2,1)S(1)} %bitcast.16), channel_id=1, source_target_pairs={{0,2},{1,3},{2,0},{3,1},{4,6},{5,7},{6,4},{7,5},{8,10},{9,11},{10,... | collective-permute-start | bytes 1572872 | tf_op jit(solution)/shard_map/ppermute | solution.py:21
  15.5 4.7 %collective-permute-done.6.refs_10_ = bf16[512,256]{1,0:T(8,128)(2,1)} collective-permute-done((bf16[512,256]{1,0:T(8,128)(2,1)S(1)}, bf16[512,256]{1,0:T(8,128)(2,1)}, u32[]{:S(2)}, u32[]{:S(2)}) %collective-permute-start.6) | collective-permute-done | bytes 262176 | tf_op jit(solution)/shard_map/ppermute | solution.py:36
  20.2 1.6 %collective-permute-start.8 = (bf16[512,256]{1,0:T(8,128)(2,1)}, bf16[512,256]{1,0:T(8,128)(2,1)}, u32[]{:S(2)}, u32[]{:S(2)}) collective-permute-start(bf16[512,256]{1,0:T(8,128)(2,1)} %collective-permute-done.6.refs_10_), channel_id=1, source_target_pairs={{0,8},{1,5},{2,10},{3,7},{8,16},{9,1},{10,18},{11,3},{16,24},{17,9... | collective-permute-start | bytes 786440 | tf_op jit(solution)/shard_map/ppermute | solution.py:36
  21.8 1.6 %collective-permute-start.5 = (bf16[512,256]{1,0:T(8,128)(2,1)}, bf16[512,256]{1,0:T(8,128)(2,1)S(1)}, u32[]{:S(2)}, u32[]{:S(2)}) collective-permute-start(bf16[512,256]{1,0:T(8,128)(2,1)} %copy-done.1), channel_id=1, source_target_pairs={{0,1},{1,0},{2,3},{3,2},{4,5},{5,4},{6,7},{7,6},{8,9},{9,8},{10,11... | collective-permute-start | bytes 786440 | tf_op jit(solution)/shard_map/ppermute | solution.py:21
  23.4 5.2 %collective-permute-done.8.refs_12_ = bf16[512,256]{1,0:T(8,128)(2,1)} collective-permute-done((bf16[512,256]{1,0:T(8,128)(2,1)}, bf16[512,256]{1,0:T(8,128)(2,1)}, u32[]{:S(2)}, u32[]{:S(2)}) %collective-permute-start.8) | collective-permute-done | bytes 262176 | tf_op jit(solution)/shard_map/ppermute | solution.py:36
  28.6 1.6 %collective-permute-start.15 = (bf16[512,512]{1,0:T(8,128)(2,1)}, bf16[512,512]{1,0:T(8,128)(2,1)}, u32[]{:S(2)}, u32[]{:S(2)}) collective-permute-start(bf16[512,512]{1,0:T(8,128)(2,1)} %collective-permute-done.13.refs_8_), channel_id=1, source_target_pairs={{0,8},{1,5},{2,10},{3,7},{8,16},{9,1},{10,18},{11,3},{16,24},{17,9... | collective-permute-start | bytes 1572872 | tf_op jit(solution)/shard_map/ppermute | solution.py:36
  30.2 0.9 constant_dynamic-slice_fusion.2
  31.1 1.6 %collective-permute-start.29 = (bf16[512,512]{1,0:T(8,128)(2,1)}, bf16[512,512]{1,0:T(8,128)(2,1)}, u32[]{:S(2)}, u32[]{:S(2)}) collective-permute-start(bf16[512,512]{1,0:T(8,128)(2,1)} %collective-permute-done.27.refs_1_), channel_id=1, source_target_pairs={{0,8},{1,5},{2,10},{3,7},{8,16},{9,1},{10,18},{11,3},{16,24},{17,9... | collective-permute-start | bytes 1572872 | tf_op jit(solution)/shard_map/ppermute | solution.py:36
  32.8 1.5 %collective-permute-start.10 = (bf16[256,256]{1,0:T(8,128)(2,1)S(1)}, bf16[256,256]{1,0:T(8,128)(2,1)S(1)}, u32[]{:S(2)}, u32[]{:S(2)}) collective-permute-start(bf16[256,256]{1,0:T(8,128)(2,1)S(1)} %constant_dynamic-slice_fusion.2), channel_id=1, source_target_pairs={{0,8},{1,5},{2,10},{3,7},{8,16},{9,1},{10,18},{11,3},{16,24},{17,9... | collective-permute-start | bytes 393224 | tf_op jit(solution)/shard_map/ppermute | solution.py:36
  34.3 2.6 %collective-permute-done.2.refs_6_ = bf16[256,1024]{1,0:T(8,128)(2,1)S(1)} collective-permute-done((bf16[256,1024]{1,0:T(8,128)(2,1)}, bf16[256,1024]{1,0:T(8,128)(2,1)S(1)}, u32[]{:S(2)}, u32[]{:S(2)}) %collective-permute-start.2) | collective-permute-done | bytes 524320 | tf_op jit(solution)/shard_map/ppermute | solution.py:21
  36.9 1.1 collective-permute-start.7
  38.0 7.0 %collective-permute-done.10.refs_14_ = bf16[256,256]{1,0:T(8,128)(2,1)S(1)} collective-permute-done((bf16[256,256]{1,0:T(8,128)(2,1)S(1)}, bf16[256,256]{1,0:T(8,128)(2,1)S(1)}, u32[]{:S(2)}, u32[]{:S(2)}) %collective-permute-start.10) | collective-permute-done | bytes 131104 | tf_op jit(solution)/shard_map/ppermute | solution.py:36
  45.6 1.6 %collective-permute-start.17 = (bf16[512,512]{1,0:T(8,128)(2,1)}, bf16[512,512]{1,0:T(8,128)(2,1)}, u32[]{:S(2)}, u32[]{:S(2)}) collective-permute-start(bf16[512,512]{1,0:T(8,128)(2,1)} %collective-permute-done.15.refs_10_), channel_id=1, source_target_pairs={{0,8},{1,5},{2,10},{3,7},{8,16},{9,1},{10,18},{11,3},{16,24},{17,9... | collective-permute-start | bytes 1572872 | tf_op jit(solution)/shard_map/ppermute | solution.py:36
  47.2 0.8 broadcast_multiply_fusion
  48.0 1.6 %collective-permute-start.31 = (bf16[512,512]{1,0:T(8,128)(2,1)}, bf16[512,512]{1,0:T(8,128)(2,1)}, u32[]{:S(2)}, u32[]{:S(2)}) collective-permute-start(bf16[512,512]{1,0:T(8,128)(2,1)} %collective-permute-done.29.refs_1_), channel_id=1, source_target_pairs={{0,8},{1,5},{2,10},{3,7},{8,16},{9,1},{10,18},{11,3},{16,24},{17,9... | collective-permute-start | bytes 1572872 | tf_op jit(solution)/shard_map/ppermute | solution.py:36
  49.6 2.8 %shard_map.82 = (bf16[256,256]{1,0:T(8,128)(2,1)}, f32[256,128]{1,0:T(8,128)S(1)}) custom-call(f32[256,128]{1,0:T(8,128)S(1)} %get-tuple-element.34.refs_0_.refs_1_, f32[256,128]{1,0:T(8,128)S(1)} %get-tuple-element.34.refs_0_.refs_1_, f32[256,128]{1,0:T(8,128)S(1)} %get-tuple-element.26.refs_2_, bf16[256,1024]{1,0:T(8,128)(2,1)S(1)} %bitcast.17, ...), custom_call_target="tpu_custom_call" | custom-call | flops 536870912 | bytes 4194304 | tf_op jit(solution)/shard_map/pallas_call | solution.py:126
  52.5 0.6 copy-done.3
  53.6 0.6 collective-permute-start.14
  54.9 8.5 %collective-permute-done.22 = bf16[256,256]{1,0:T(8,128)(2,1)S(1)} collective-permute-done((bf16[256,256]{1,0:T(8,128)(2,1)}, bf16[256,256]{1,0:T(8,128)(2,1)S(1)}, u32[]{:S(2)}, u32[]{:S(2)}) %collective-permute-start.22) | collective-permute-done | bytes 131104 | tf_op jit(solution)/shard_map/ppermute | solution.py:21
  63.5 0.9 broadcast_select_fusion
  64.6 1.0 constant_dynamic-slice_fusion.1
  65.6 2.0 %collective-permute-start.19 = (bf16[256,512]{1,0:T(8,128)(2,1)S(1)}, bf16[256,512]{1,0:T(8,128)(2,1)}, u32[]{:S(2)}, u32[]{:S(2)}) collective-permute-start(bf16[256,512]{1,0:T(8,128)(2,1)S(1)} %constant_dynamic-slice_fusion.1), channel_id=1, source_target_pairs={{0,8},{1,5},{2,10},{3,7},{8,16},{9,1},{10,18},{11,3},{16,24},{17,9... | collective-permute-start | bytes 786440 | tf_op jit(solution)/shard_map/ppermute | solution.py:36
  67.5 1.7 %constant_dynamic-slice_fusion = bf16[256,512]{1,0:T(8,128)(2,1)} fusion(bf16[512,512]{1,0:T(8,128)(2,1)} %collective-permute-done.31.refs_1_, s32[]{:T(128)S(6)} %select_n.102), kind=kLoop, calls=%fused_computation.23 | loop fusion | bytes 524292 | tf_op jit(solution)/shard_map/dynamic_slice | solution.py:47
  69.2 1.7 %collective-permute-start.33 = (bf16[256,512]{1,0:T(8,128)(2,1)}, bf16[256,512]{1,0:T(8,128)(2,1)S(1)}, u32[]{:S(2)}, u32[]{:S(2)}) collective-permute-start(bf16[256,512]{1,0:T(8,128)(2,1)} %constant_dynamic-slice_fusion), channel_id=1, source_target_pairs={{0,8},{1,5},{2,10},{3,7},{8,16},{9,1},{10,18},{11,3},{16,24},{17,9... | collective-permute-start | bytes 786440 | tf_op jit(solution)/shard_map/ppermute | solution.py:36
  70.9 0.7 broadcast_select_fusion.1
  71.6 0.7 copy-done.5
  72.8 9.3 %collective-permute-done.24 = bf16[256,256]{1,0:T(8,128)(2,1)} collective-permute-done((bf16[256,256]{1,0:T(8,128)(2,1)}, bf16[256,256]{1,0:T(8,128)(2,1)}, u32[]{:S(2)}, u32[]{:S(2)}) %collective-permute-start.24) | collective-permute-done | bytes 131104 | tf_op jit(solution)/shard_map/ppermute | solution.py:21
  82.6 0.9 broadcast_select_fusion.2.far0
  84.2 3.7 %shard_map.83.q_ref = bf16[256,512]{1,0:T(8,128)(2,1)S(1)} custom-call(f32[256,128]{1,0:T(8,128)S(1)} %copy-done.4, f32[256,128]{1,0:T(8,128)S(1)} %copy-done, f32[256,128]{1,0:T(8,128)S(1)} %get-tuple-element.25.refs_2_, bf16[256,1024]{1,0:T(8,128)(2,1)S(1)} %bitcast.18, bf16[256,1024]{1,0:T(8,128)(2,1)S(1)} %collective-permute-done.refs_4_, ...), custom_call_target="tpu_custom_call" | custom-call | flops 1073741824 | bytes 6291456 | tf_op jit(solution)/shard_map/pallas_call | solution.py:126
  88.0 3.2 %shard_map.84.a_ref = bf16[256,512]{1,0:T(8,128)(2,1)S(1)} custom-call(s32[4,4]{1,0:T(4,128)S(1)} %bitcast.19, s32[4,4]{1,0:T(4,128)S(1)} %select_bitcast_fusion.far_ref, bf16[256,512]{1,0:T(8,128)(2,1)S(1)} %shard_map.83.q_ref, bf16[256,256]{1,0:T(8,128)(2,1)} %get-tuple-element.16.near0, bf16[256,256]{1,0:T(8,128)(2,1)S(1)} %copy-done.6, ...), custom_call_target="tpu_custom_call" | custom-call | flops 536870912 | bytes 1048576 | tf_op jit(solution)/shard_map/pallas_call | solution.py:210
  91.2 1.5 %shard_map.85 = (f32[128,1024]{1,0:T(8,128)S(1)}, bf16[128,1024]{1,0:T(8,128)(2,1)S(1)}) custom-call(bf16[256,512]{1,0:T(8,128)(2,1)S(1)} %shard_map.84.a_ref, bf16[512,512]{1,0:T(8,128)(2,1)S(1)} %maximum_select_fusion.1.refs_0_, bf16[512,512]{1,0:T(8,128)(2,1)} %collective-permute-done.27.refs_1_), custom_call_target="tpu_custom_call" | custom-call | flops 268435456 | bytes 2097152 | tf_op jit(solution)/shard_map/pallas_call | solution.py:256
  92.7 1.6 %collective-permute-start.35 = (bf16[128,1024]{1,0:T(8,128)(2,1)S(1)}, bf16[128,1024]{1,0:T(8,128)(2,1)S(1)}, u32[]{:S(2)}, u32[]{:S(2)}) collective-permute-start(bf16[128,1024]{1,0:T(8,128)(2,1)S(1)} %get-tuple-element.21), channel_id=1, source_target_pairs={{0,2},{1,3},{2,0},{3,1},{4,6},{5,7},{6,4},{7,5},{8,10},{9,11},{10,... | collective-permute-start | bytes 786440 | tf_op jit(solution)/shard_map/ppermute | solution.py:21
  94.3 1.5 %shard_map.86 = (f32[128,1024]{1,0:T(8,128)S(1)}, bf16[128,1024]{1,0:T(8,128)(2,1)S(1)}) custom-call(bf16[256,512]{1,0:T(8,128)(2,1)S(1)} %shard_map.84.a_ref, bf16[512,512]{1,0:T(8,128)(2,1)S(1)} %collective-permute-done.28.refs_0_, bf16[512,512]{1,0:T(8,128)(2,1)} %collective-permute-done.29.refs_1_), custom_call_target="tpu_custom_call" | custom-call | flops 268435456 | bytes 2097152 | tf_op jit(solution)/shard_map/pallas_call | solution.py:256
  95.8 0.6 collective-permute-start.36
  96.4 1.5 %shard_map.87 = (f32[128,1024]{1,0:T(8,128)S(1)}, bf16[128,1024]{1,0:T(8,128)(2,1)S(1)}) custom-call(bf16[256,512]{1,0:T(8,128)(2,1)S(1)} %shard_map.84.a_ref, bf16[512,512]{1,0:T(8,128)(2,1)S(1)} %collective-permute-done.30.refs_0_, bf16[512,512]{1,0:T(8,128)(2,1)} %collective-permute-done.31.refs_1_), custom_call_target="tpu_custom_call" | custom-call | flops 268435456 | bytes 2097152 | tf_op jit(solution)/shard_map/pallas_call | solution.py:256
  97.9 1.6 %collective-permute-start.37 = (bf16[128,1024]{1,0:T(8,128)(2,1)S(1)}, bf16[128,1024]{1,0:T(8,128)(2,1)S(1)}, u32[]{:S(2)}, u32[]{:S(2)}) collective-permute-start(bf16[128,1024]{1,0:T(8,128)(2,1)S(1)} %get-tuple-element.23), channel_id=1, source_target_pairs={{0,2},{1,3},{2,0},{3,1},{4,6},{5,7},{6,4},{7,5},{8,10},{9,11},{10,... | collective-permute-start | bytes 786440 | tf_op jit(solution)/shard_map/ppermute | solution.py:21
  100.7 1.2 %collective-permute-done.35.refs_4_ = bf16[128,1024]{1,0:T(8,128)(2,1)S(1)} collective-permute-done((bf16[128,1024]{1,0:T(8,128)(2,1)S(1)}, bf16[128,1024]{1,0:T(8,128)(2,1)S(1)}, u32[]{:S(2)}, u32[]{:S(2)}) %collective-permute-start.35) | collective-permute-done | bytes 262176 | tf_op jit(solution)/shard_map/ppermute | solution.py:21
  101.9 5.6 %collective-permute-done.36.refs_5_ = bf16[128,1024]{1,0:T(8,128)(2,1)S(1)} collective-permute-done((bf16[128,1024]{1,0:T(8,128)(2,1)S(1)}, bf16[128,1024]{1,0:T(8,128)(2,1)S(1)}, u32[]{:S(2)}, u32[]{:S(2)}) %collective-permute-start.36) | collective-permute-done | bytes 262176 | tf_op jit(solution)/shard_map/ppermute | solution.py:21
  107.5 5.6 %collective-permute-done.37.refs_6_ = bf16[128,1024]{1,0:T(8,128)(2,1)S(1)} collective-permute-done((bf16[128,1024]{1,0:T(8,128)(2,1)S(1)}, bf16[128,1024]{1,0:T(8,128)(2,1)S(1)}, u32[]{:S(2)}, u32[]{:S(2)}) %collective-permute-start.37) | collective-permute-done | bytes 262176 | tf_op jit(solution)/shard_map/ppermute | solution.py:21
  113.1 5.2 %collective-permute-done.38.refs_7_ = bf16[128,1024]{1,0:T(8,128)(2,1)S(1)} collective-permute-done((bf16[128,1024]{1,0:T(8,128)(2,1)S(1)}, bf16[128,1024]{1,0:T(8,128)(2,1)S(1)}, u32[]{:S(2)}, u32[]{:S(2)}) %collective-permute-start.38) | collective-permute-done | bytes 262176 | tf_op jit(solution)/shard_map/ppermute | solution.py:21
  118.3 1.1 shard_map.89
  (76 shorter events, 5.8 us)
Async XLA Ops:
  0.0 1.7 %collective-permute-start.3 = (bf16[512,128]{1,0:T(8,128)(2,1)}, bf16[512,128]{1,0:T(8,128)(2,1)S(1)}, u32[]{:S(2)}, u32[]{:S(2)}) collective-permute-start(bf16[512,128]{1,0:T(8,128)(2,1)} %bitcast.21), channel_id=1, source_target_pairs={{0,1},{1,0},{2,3},{3,2},{4,5},{5,4},{6,7},{7,6},{8,9},{9,8},{10,11... | collective-permute-start | bytes 393224 | tf_op jit(solution)/shard_map/ppermute | solution.py:21
  0.5 7.4 %collective-permute-start.12 = (bf16[512,256]{1,0:T(8,128)(2,1)}, bf16[512,256]{1,0:T(8,128)(2,1)S(1)}, u32[]{:S(2)}, u32[]{:S(2)}) collective-permute-start(bf16[512,256]{1,0:T(8,128)(2,1)} %param.10), channel_id=1, source_target_pairs={{0,1},{1,0},{2,3},{3,2},{4,5},{5,4},{6,7},{7,6},{8,9},{9,8},{10,11... | collective-permute-start | bytes 786440 | tf_op jit(solution)/shard_map/ppermute | solution.py:21
  0.5 11.6 %collective-permute-start.26 = (bf16[256,512]{1,0:T(8,128)(2,1)}, bf16[256,512]{1,0:T(8,128)(2,1)S(1)}, u32[]{:S(2)}, u32[]{:S(2)}) collective-permute-start(bf16[256,512]{1,0:T(8,128)(2,1)} %param.12), channel_id=1, source_target_pairs={{0,1},{1,0},{2,3},{3,2},{4,5},{5,4},{6,7},{7,6},{8,9},{9,8},{10,11... | collective-permute-start | bytes 786440 | tf_op jit(solution)/shard_map/ppermute | solution.py:21
  2.8 7.2 %collective-permute-start.4 = (bf16[512,256]{1,0:T(8,128)(2,1)S(1)}, bf16[512,256]{1,0:T(8,128)(2,1)S(1)}, u32[]{:S(2)}, u32[]{:S(2)}) collective-permute-start(bf16[512,256]{1,0:T(8,128)(2,1)S(1)} %multiply_convert_fusion.1.refs_7_), channel_id=1, source_target_pairs={{0,8},{1,5},{2,10},{3,7},{8,16},{9,1},{10,18},{11,3},{16,24},{17,9... | collective-permute-start | bytes 786440 | tf_op jit(solution)/shard_map/ppermute | solution.py:36
  5.8 2.1 %copy-start.8 = (bf16[512,256]{1,0:T(8,128)(2,1)S(1)}, bf16[512,256]{1,0:T(8,128)(2,1)}, u32[]{:S(2)}) copy-start(bf16[512,256]{1,0:T(8,128)(2,1)} %param.10) | copy-start | bytes 786436
  7.9 4.2 %copy-start.9 = (bf16[256,512]{1,0:T(8,128)(2,1)S(1)}, bf16[256,512]{1,0:T(8,128)(2,1)}, u32[]{:S(2)}) copy-start(bf16[256,512]{1,0:T(8,128)(2,1)} %param.12) | copy-start | bytes 786436
  7.9 13.9 %collective-permute-start = (bf16[256,1024]{1,0:T(8,128)(2,1)}, bf16[256,1024]{1,0:T(8,128)(2,1)S(1)}, u32[]{:S(2)}, u32[]{:S(2)}) collective-permute-start(bf16[256,1024]{1,0:T(8,128)(2,1)} %bitcast.5), channel_id=1, source_target_pairs={{0,1},{1,0},{2,3},{3,2},{4,5},{5,4},{6,7},{7,6},{8,9},{9,8},{10,11... | collective-permute-start | bytes 1572872 | tf_op jit(solution)/shard_map/ppermute | solution.py:21
  8.1 13.7 %collective-permute-start.13 = (bf16[512,512]{1,0:T(8,128)(2,1)S(1)}, bf16[512,512]{1,0:T(8,128)(2,1)}, u32[]{:S(2)}, u32[]{:S(2)}) collective-permute-start(bf16[512,512]{1,0:T(8,128)(2,1)S(1)} %multiply_convert_fusion.refs_7_), channel_id=1, source_target_pairs={{0,8},{1,5},{2,10},{3,7},{8,16},{9,1},{10,18},{11,3},{16,24},{17,9... | collective-permute-start | bytes 1572872 | tf_op jit(solution)/shard_map/ppermute | solution.py:36
  10.0 2.3 %copy-start.1 = (bf16[512,256]{1,0:T(8,128)(2,1)}, bf16[512,256]{1,0:T(8,128)(2,1)S(1)}, u32[]{:S(2)}) copy-start(bf16[512,256]{1,0:T(8,128)(2,1)S(1)} %collective-permute-done.4.refs_8_) | copy-start | bytes 786436
  10.0 10.2 %collective-permute-start.6 = (bf16[512,256]{1,0:T(8,128)(2,1)S(1)}, bf16[512,256]{1,0:T(8,128)(2,1)}, u32[]{:S(2)}, u32[]{:S(2)}) collective-permute-start(bf16[512,256]{1,0:T(8,128)(2,1)S(1)} %collective-permute-done.4.refs_8_), channel_id=1, source_target_pairs={{0,8},{1,5},{2,10},{3,7},{8,16},{9,1},{10,18},{11,3},{16,24},{17,9... | collective-permute-start | bytes 786440 | tf_op jit(solution)/shard_map/ppermute | solution.py:36
  12.4 18.8 %collective-permute-start.27 = (bf16[512,512]{1,0:T(8,128)(2,1)S(1)}, bf16[512,512]{1,0:T(8,128)(2,1)}, u32[]{:S(2)}, u32[]{:S(2)}) collective-permute-start(bf16[512,512]{1,0:T(8,128)(2,1)S(1)} %maximum_select_fusion.1.refs_0_), channel_id=1, source_target_pairs={{0,8},{1,5},{2,10},{3,7},{8,16},{9,1},{10,18},{11,3},{16,24},{17,9... | collective-permute-start | bytes 1572872 | tf_op jit(solution)/shard_map/ppermute | solution.py:36
  14.0 18.8 %collective-permute-start.1 = (bf16[256,1024]{1,0:T(8,128)(2,1)S(1)}, bf16[256,1024]{1,0:T(8,128)(2,1)S(1)}, u32[]{:S(2)}, u32[]{:S(2)}) collective-permute-start(bf16[256,1024]{1,0:T(8,128)(2,1)S(1)} %bitcast.16), channel_id=1, source_target_pairs={{0,2},{1,3},{2,0},{3,1},{4,6},{5,7},{6,4},{7,5},{8,10},{9,11},{10,... | collective-permute-start | bytes 1572872 | tf_op jit(solution)/shard_map/ppermute | solution.py:21
  20.2 8.4 %collective-permute-start.8 = (bf16[512,256]{1,0:T(8,128)(2,1)}, bf16[512,256]{1,0:T(8,128)(2,1)}, u32[]{:S(2)}, u32[]{:S(2)}) collective-permute-start(bf16[512,256]{1,0:T(8,128)(2,1)} %collective-permute-done.6.refs_10_), channel_id=1, source_target_pairs={{0,8},{1,5},{2,10},{3,7},{8,16},{9,1},{10,18},{11,3},{16,24},{17,9... | collective-permute-start | bytes 786440 | tf_op jit(solution)/shard_map/ppermute | solution.py:36
  21.8 15.1 %collective-permute-start.2 = (bf16[256,1024]{1,0:T(8,128)(2,1)}, bf16[256,1024]{1,0:T(8,128)(2,1)S(1)}, u32[]{:S(2)}, u32[]{:S(2)}) collective-permute-start(bf16[256,1024]{1,0:T(8,128)(2,1)} %bitcast.5), channel_id=1, source_target_pairs={{0,3},{1,2},{2,1},{3,0},{4,7},{5,6},{6,5},{7,4},{8,11},{9,10},{10,... | collective-permute-start | bytes 1572872 | tf_op jit(solution)/shard_map/ppermute | solution.py:21
  21.8 16.2 %collective-permute-start.5 = (bf16[512,256]{1,0:T(8,128)(2,1)}, bf16[512,256]{1,0:T(8,128)(2,1)S(1)}, u32[]{:S(2)}, u32[]{:S(2)}) collective-permute-start(bf16[512,256]{1,0:T(8,128)(2,1)} %copy-done.1), channel_id=1, source_target_pairs={{0,1},{1,0},{2,3},{3,2},{4,5},{5,4},{6,7},{7,6},{8,9},{9,8},{10,11... | collective-permute-start | bytes 786440 | tf_op jit(solution)/shard_map/ppermute | solution.py:21
  28.6 17.0 %collective-permute-start.15 = (bf16[512,512]{1,0:T(8,128)(2,1)}, bf16[512,512]{1,0:T(8,128)(2,1)}, u32[]{:S(2)}, u32[]{:S(2)}) collective-permute-start(bf16[512,512]{1,0:T(8,128)(2,1)} %collective-permute-done.13.refs_8_), channel_id=1, source_target_pairs={{0,8},{1,5},{2,10},{3,7},{8,16},{9,1},{10,18},{11,3},{16,24},{17,9... | collective-permute-start | bytes 1572872 | tf_op jit(solution)/shard_map/ppermute | solution.py:36
  31.1 16.9 %collective-permute-start.29 = (bf16[512,512]{1,0:T(8,128)(2,1)}, bf16[512,512]{1,0:T(8,128)(2,1)}, u32[]{:S(2)}, u32[]{:S(2)}) collective-permute-start(bf16[512,512]{1,0:T(8,128)(2,1)} %collective-permute-done.27.refs_1_), channel_id=1, source_target_pairs={{0,8},{1,5},{2,10},{3,7},{8,16},{9,1},{10,18},{11,3},{16,24},{17,9... | collective-permute-start | bytes 1572872 | tf_op jit(solution)/shard_map/ppermute | solution.py:36
  32.8 12.3 %collective-permute-start.10 = (bf16[256,256]{1,0:T(8,128)(2,1)S(1)}, bf16[256,256]{1,0:T(8,128)(2,1)S(1)}, u32[]{:S(2)}, u32[]{:S(2)}) collective-permute-start(bf16[256,256]{1,0:T(8,128)(2,1)S(1)} %constant_dynamic-slice_fusion.2), channel_id=1, source_target_pairs={{0,8},{1,5},{2,10},{3,7},{8,16},{9,1},{10,18},{11,3},{16,24},{17,9... | collective-permute-start | bytes 393224 | tf_op jit(solution)/shard_map/ppermute | solution.py:36
  36.9 12.7 %collective-permute-start.7 = (bf16[512,256]{1,0:T(8,128)(2,1)}, bf16[512,256]{1,0:T(8,128)(2,1)S(1)}, u32[]{:S(2)}, u32[]{:S(2)}) collective-permute-start(bf16[512,256]{1,0:T(8,128)(2,1)} %collective-permute-done.6.refs_10_), channel_id=1, source_target_pairs={{0,1},{1,0},{2,3},{3,2},{4,5},{5,4},{6,7},{7,6},{8,9},{9,8},{10,11... | collective-permute-start | bytes 786440 | tf_op jit(solution)/shard_map/ppermute | solution.py:21
  38.0 11.6 %collective-permute-start.9 = (bf16[512,256]{1,0:T(8,128)(2,1)}, bf16[512,256]{1,0:T(8,128)(2,1)S(1)}, u32[]{:S(2)}, u32[]{:S(2)}) collective-permute-start(bf16[512,256]{1,0:T(8,128)(2,1)} %collective-permute-done.8.refs_12_), channel_id=1, source_target_pairs={{0,1},{1,0},{2,3},{3,2},{4,5},{5,4},{6,7},{7,6},{8,9},{9,8},{10,11... | collective-permute-start | bytes 786440 | tf_op jit(solution)/shard_map/ppermute | solution.py:21
  45.0 4.5 %collective-permute-start.11 = (bf16[256,256]{1,0:T(8,128)(2,1)S(1)}, bf16[256,256]{1,0:T(8,128)(2,1)S(1)}, u32[]{:S(2)}, u32[]{:S(2)}) collective-permute-start(bf16[256,256]{1,0:T(8,128)(2,1)S(1)} %collective-permute-done.10.refs_14_), channel_id=1, source_target_pairs={{0,1},{1,0},{2,3},{3,2},{4,5},{5,4},{6,7},{7,6},{8,9},{9,8},{10,11... | collective-permute-start | bytes 393224 | tf_op jit(solution)/shard_map/ppermute | solution.py:21
  45.6 18.9 %collective-permute-start.17 = (bf16[512,512]{1,0:T(8,128)(2,1)}, bf16[512,512]{1,0:T(8,128)(2,1)}, u32[]{:S(2)}, u32[]{:S(2)}) collective-permute-start(bf16[512,512]{1,0:T(8,128)(2,1)} %collective-permute-done.15.refs_10_), channel_id=1, source_target_pairs={{0,8},{1,5},{2,10},{3,7},{8,16},{9,1},{10,18},{11,3},{16,24},{17,9... | collective-permute-start | bytes 1572872 | tf_op jit(solution)/shard_map/ppermute | solution.py:36
  47.2 2.4 %copy-start.2 = (bf16[512,256]{1,0:T(8,128)(2,1)S(1)}, bf16[512,256]{1,0:T(8,128)(2,1)}, u32[]{:S(2)}) copy-start(bf16[512,256]{1,0:T(8,128)(2,1)} %copy-done.1) | copy-start | bytes 786436
  48.0 17.5 %collective-permute-start.31 = (bf16[512,512]{1,0:T(8,128)(2,1)}, bf16[512,512]{1,0:T(8,128)(2,1)}, u32[]{:S(2)}, u32[]{:S(2)}) collective-permute-start(bf16[512,512]{1,0:T(8,128)(2,1)} %collective-permute-done.29.refs_1_), channel_id=1, source_target_pairs={{0,8},{1,5},{2,10},{3,7},{8,16},{9,1},{10,18},{11,3},{16,24},{17,9... | collective-permute-start | bytes 1572872 | tf_op jit(solution)/shard_map/ppermute | solution.py:36
  53.1 10.4 %collective-permute-start.22 = (bf16[256,256]{1,0:T(8,128)(2,1)}, bf16[256,256]{1,0:T(8,128)(2,1)S(1)}, u32[]{:S(2)}, u32[]{:S(2)}) collective-permute-start(bf16[256,256]{1,0:T(8,128)(2,1)} %get-tuple-element.16.near0), channel_id=1, source_target_pairs={{0,4},{4,0},{8,12},{12,8},{16,20},{20,16},{24,28},{28,24},{1,5},{5... | collective-permute-start | bytes 393224 | tf_op jit(solution)/shard_map/ppermute | solution.py:21
  53.6 15.6 %collective-permute-start.14 = (bf16[512,512]{1,0:T(8,128)(2,1)}, bf16[512,512]{1,0:T(8,128)(2,1)}, u32[]{:S(2)}, u32[]{:S(2)}) collective-permute-start(bf16[512,512]{1,0:T(8,128)(2,1)} %collective-permute-done.13.refs_8_), channel_id=1, source_target_pairs={{0,1},{1,0},{2,3},{3,2},{4,5},{5,4},{6,7},{7,6},{8,9},{9,8},{10,11... | collective-permute-start | bytes 1572872 | tf_op jit(solution)/shard_map/ppermute | solution.py:21
  54.9 16.7 %collective-permute-start.21 = (bf16[256,256]{1,0:T(8,128)(2,1)}, bf16[256,256]{1,0:T(8,128)(2,1)S(1)}, u32[]{:S(2)}, u32[]{:S(2)}) collective-permute-start(bf16[256,256]{1,0:T(8,128)(2,1)} %get-tuple-element.16.near0), channel_id=1, source_target_pairs={{0,1},{1,0},{2,3},{3,2},{4,5},{5,4},{6,7},{7,6},{8,9},{9,8},{10,11... | collective-permute-start | bytes 393224 | tf_op jit(solution)/shard_map/ppermute | solution.py:21
  64.4 6.5 %collective-permute-start.23 = (bf16[256,256]{1,0:T(8,128)(2,1)S(1)}, bf16[256,256]{1,0:T(8,128)(2,1)S(1)}, u32[]{:S(2)}, u32[]{:S(2)}) collective-permute-start(bf16[256,256]{1,0:T(8,128)(2,1)S(1)} %broadcast_select_fusion), channel_id=1, source_target_pairs={{0,8},{4,12},{8,0},{12,4},{16,24},{20,28},{24,16},{28,20},{1,9},{5... | collective-permute-start | bytes 393224 | tf_op jit(solution)/shard_map/ppermute | solution.py:21
  64.5 17.6 %collective-permute-start.16 = (bf16[512,512]{1,0:T(8,128)(2,1)}, bf16[512,512]{1,0:T(8,128)(2,1)}, u32[]{:S(2)}, u32[]{:S(2)}) collective-permute-start(bf16[512,512]{1,0:T(8,128)(2,1)} %collective-permute-done.15.refs_10_), channel_id=1, source_target_pairs={{0,1},{1,0},{2,3},{3,2},{4,5},{5,4},{6,7},{7,6},{8,9},{9,8},{10,11... | collective-permute-start | bytes 1572872 | tf_op jit(solution)/shard_map/ppermute | solution.py:21
  65.6 6.7 %collective-permute-start.19 = (bf16[256,512]{1,0:T(8,128)(2,1)S(1)}, bf16[256,512]{1,0:T(8,128)(2,1)}, u32[]{:S(2)}, u32[]{:S(2)}) collective-permute-start(bf16[256,512]{1,0:T(8,128)(2,1)S(1)} %constant_dynamic-slice_fusion.1), channel_id=1, source_target_pairs={{0,8},{1,5},{2,10},{3,7},{8,16},{9,1},{10,18},{11,3},{16,24},{17,9... | collective-permute-start | bytes 786440 | tf_op jit(solution)/shard_map/ppermute | solution.py:36
  69.2 13.3 %collective-permute-start.33 = (bf16[256,512]{1,0:T(8,128)(2,1)}, bf16[256,512]{1,0:T(8,128)(2,1)S(1)}, u32[]{:S(2)}, u32[]{:S(2)}) collective-permute-start(bf16[256,512]{1,0:T(8,128)(2,1)} %constant_dynamic-slice_fusion), channel_id=1, source_target_pairs={{0,8},{1,5},{2,10},{3,7},{8,16},{9,1},{10,18},{11,3},{16,24},{17,9... | collective-permute-start | bytes 786440 | tf_op jit(solution)/shard_map/ppermute | solution.py:36
  70.9 13.2 %collective-permute-start.18 = (bf16[512,512]{1,0:T(8,128)(2,1)}, bf16[512,512]{1,0:T(8,128)(2,1)}, u32[]{:S(2)}, u32[]{:S(2)}) collective-permute-start(bf16[512,512]{1,0:T(8,128)(2,1)} %collective-permute-done.17.refs_12_), channel_id=1, source_target_pairs={{0,1},{1,0},{2,3},{3,2},{4,5},{5,4},{6,7},{7,6},{8,9},{9,8},{10,11... | collective-permute-start | bytes 1572872 | tf_op jit(solution)/shard_map/ppermute | solution.py:21
  72.2 9.8 %collective-permute-start.24 = (bf16[256,256]{1,0:T(8,128)(2,1)}, bf16[256,256]{1,0:T(8,128)(2,1)}, u32[]{:S(2)}, u32[]{:S(2)}) collective-permute-start(bf16[256,256]{1,0:T(8,128)(2,1)} %broadcast_select_fusion.1), channel_id=1, source_target_pairs={{0,16},{4,20},{8,24},{12,28},{16,0},{20,4},{24,8},{28,12},{1,17},{... | collective-permute-start | bytes 393224 | tf_op jit(solution)/shard_map/ppermute | solution.py:21
  72.3 11.3 %collective-permute-start.20 = (bf16[256,512]{1,0:T(8,128)(2,1)}, bf16[256,512]{1,0:T(8,128)(2,1)}, u32[]{:S(2)}, u32[]{:S(2)}) collective-permute-start(bf16[256,512]{1,0:T(8,128)(2,1)} %collective-permute-done.19.refs_14_), channel_id=1, source_target_pairs={{0,1},{1,0},{2,3},{3,2},{4,5},{5,4},{6,7},{7,6},{8,9},{9,8},{10,11... | collective-permute-start | bytes 786440 | tf_op jit(solution)/shard_map/ppermute | solution.py:21
  72.7 11.4 %copy-start.10 = (s32[1,4,4]{2,1,0:T(4,128)S(1)}, s32[1,4,4]{2,1,0:T(4,128)}, u32[]{:S(2)}) copy-start(s32[1,4,4]{2,1,0:T(4,128)} %param.14) | copy-start | bytes 196
  72.8 11.4 %copy-start = (f32[256,128]{1,0:T(8,128)S(1)}, f32[256,128]{1,0:T(8,128)}, u32[]{:S(2)}) copy-start(f32[256,128]{1,0:T(8,128)} %get-tuple-element.35.refs_1_) | copy-start | bytes 393220
  72.8 11.4 %copy-start.4 = (f32[256,128]{1,0:T(8,128)S(1)}, f32[256,128]{1,0:T(8,128)}, u32[]{:S(2)}) copy-start(f32[256,128]{1,0:T(8,128)} %copy-done.3) | copy-start | bytes 393220
  82.0 12.3 %collective-permute-start.28 = (bf16[512,512]{1,0:T(8,128)(2,1)}, bf16[512,512]{1,0:T(8,128)(2,1)S(1)}, u32[]{:S(2)}, u32[]{:S(2)}) collective-permute-start(bf16[512,512]{1,0:T(8,128)(2,1)} %collective-permute-done.27.refs_1_), channel_id=1, source_target_pairs={{0,1},{1,0},{2,3},{3,2},{4,5},{5,4},{6,7},{7,6},{8,9},{9,8},{10,11... | collective-permute-start | bytes 1572872 | tf_op jit(solution)/shard_map/ppermute | solution.py:21
  82.1 14.3 %collective-permute-start.30 = (bf16[512,512]{1,0:T(8,128)(2,1)}, bf16[512,512]{1,0:T(8,128)(2,1)S(1)}, u32[]{:S(2)}, u32[]{:S(2)}) collective-permute-start(bf16[512,512]{1,0:T(8,128)(2,1)} %collective-permute-done.29.refs_1_), channel_id=1, source_target_pairs={{0,1},{1,0},{2,3},{3,2},{4,5},{5,4},{6,7},{7,6},{8,9},{9,8},{10,11... | collective-permute-start | bytes 1572872 | tf_op jit(solution)/shard_map/ppermute | solution.py:21
  82.6 17.0 %collective-permute-start.32 = (bf16[512,512]{1,0:T(8,128)(2,1)}, bf16[512,512]{1,0:T(8,128)(2,1)S(1)}, u32[]{:S(2)}, u32[]{:S(2)}) collective-permute-start(bf16[512,512]{1,0:T(8,128)(2,1)} %collective-permute-done.31.refs_1_), channel_id=1, source_target_pairs={{0,1},{1,0},{2,3},{3,2},{4,5},{5,4},{6,7},{7,6},{8,9},{9,8},{10,11... | collective-permute-start | bytes 1572872 | tf_op jit(solution)/shard_map/ppermute | solution.py:21
  83.6 4.4 %collective-permute-start.25 = (bf16[256,256]{1,0:T(8,128)(2,1)S(1)}, bf16[256,256]{1,0:T(8,128)(2,1)S(1)}, u32[]{:S(2)}, u32[]{:S(2)}) collective-permute-start(bf16[256,256]{1,0:T(8,128)(2,1)S(1)} %broadcast_select_fusion.2.far0), channel_id=1, source_target_pairs={{0,1},{1,0},{2,3},{3,2},{4,5},{5,4},{6,7},{7,6},{8,9},{9,8},{10,11... | collective-permute-start | bytes 393224 | tf_op jit(solution)/shard_map/ppermute | solution.py:21
  84.1 15.5 %collective-permute-start.34 = (bf16[256,512]{1,0:T(8,128)(2,1)S(1)}, bf16[256,512]{1,0:T(8,128)(2,1)S(1)}, u32[]{:S(2)}, u32[]{:S(2)}) collective-permute-start(bf16[256,512]{1,0:T(8,128)(2,1)S(1)} %collective-permute-done.33.refs_1_), channel_id=1, source_target_pairs={{0,1},{1,0},{2,3},{3,2},{4,5},{5,4},{6,7},{7,6},{8,9},{9,8},{10,11... | collective-permute-start | bytes 786440 | tf_op jit(solution)/shard_map/ppermute | solution.py:21
  84.2 3.8 %copy-start.6 = (bf16[256,256]{1,0:T(8,128)(2,1)S(1)}, bf16[256,256]{1,0:T(8,128)(2,1)}, u32[]{:S(2)}) copy-start(bf16[256,256]{1,0:T(8,128)(2,1)} %copy-done.5) | copy-start | bytes 393220
  84.2 3.8 %copy-start.7 = (s32[1,4,4]{2,1,0:T(4,128)S(1)}, s32[1,4,4]{2,1,0:T(4,128)}, u32[]{:S(2)}) copy-start(s32[1,4,4]{2,1,0:T(4,128)} %param.13) | copy-start | bytes 196
  92.7 9.2 %collective-permute-start.35 = (bf16[128,1024]{1,0:T(8,128)(2,1)S(1)}, bf16[128,1024]{1,0:T(8,128)(2,1)S(1)}, u32[]{:S(2)}, u32[]{:S(2)}) collective-permute-start(bf16[128,1024]{1,0:T(8,128)(2,1)S(1)} %get-tuple-element.21), channel_id=1, source_target_pairs={{0,2},{1,3},{2,0},{3,1},{4,6},{5,7},{6,4},{7,5},{8,10},{9,11},{10,... | collective-permute-start | bytes 786440 | tf_op jit(solution)/shard_map/ppermute | solution.py:21
  95.8 11.7 %collective-permute-start.36 = (bf16[128,1024]{1,0:T(8,128)(2,1)S(1)}, bf16[128,1024]{1,0:T(8,128)(2,1)S(1)}, u32[]{:S(2)}, u32[]{:S(2)}) collective-permute-start(bf16[128,1024]{1,0:T(8,128)(2,1)S(1)} %get-tuple-element.22), channel_id=1, source_target_pairs={{0,2},{1,3},{2,0},{3,1},{4,6},{5,7},{6,4},{7,5},{8,10},{9,11},{10,... | collective-permute-start | bytes 786440 | tf_op jit(solution)/shard_map/ppermute | solution.py:21
  97.9 15.2 %collective-permute-start.37 = (bf16[128,1024]{1,0:T(8,128)(2,1)S(1)}, bf16[128,1024]{1,0:T(8,128)(2,1)S(1)}, u32[]{:S(2)}, u32[]{:S(2)}) collective-permute-start(bf16[128,1024]{1,0:T(8,128)(2,1)S(1)} %get-tuple-element.23), channel_id=1, source_target_pairs={{0,2},{1,3},{2,0},{3,1},{4,6},{5,7},{6,4},{7,5},{8,10},{9,11},{10,... | collective-permute-start | bytes 786440 | tf_op jit(solution)/shard_map/ppermute | solution.py:21
  100.1 18.2 %collective-permute-start.38 = (bf16[128,1024]{1,0:T(8,128)(2,1)S(1)}, bf16[128,1024]{1,0:T(8,128)(2,1)S(1)}, u32[]{:S(2)}, u32[]{:S(2)}) collective-permute-start(bf16[128,1024]{1,0:T(8,128)(2,1)S(1)} %get-tuple-element.24), channel_id=1, source_target_pairs={{0,2},{1,3},{2,0},{3,1},{4,6},{5,7},{6,4},{7,5},{8,10},{9,11},{10,... | collective-permute-start | bytes 786440 | tf_op jit(solution)/shard_map/ppermute | solution.py:21
  (2 other events, 1.3 us)
where the time goes:
time: 120 us; the launch traced here: 119 us
  waiting for transfers between devices  55.4 us (46%)
  starting transfers between devices  33.9 us (28%)
  Pallas kernels  16.1 us (13%)
  local copies, waits for them, and re-layouts  7.02 us (6%)
  other arithmetic  6.06 us (5%)
    ppermute x27, waiting for transfers between devices, swap(): return lax.ppermute(value, axis, pairs)  38.1 us
    ppermute x12, starting transfers between devices, ring_step(): return lax.ppermute(value, ('ctx', 'zero'), pairs)  21.4 us
    ppermute x12, waiting for transfers between devices, ring_step(): return lax.ppermute(value, ('ctx', 'zero'), pairs)  17.3 us
    ppermute x27, starting transfers between devices, swap(): return lax.ppermute(value, axis, pairs)  12.5 us
    pallas_call x2, Pallas kernels, project(): pl.pallas_call(functools.partial(project_kernel, layout, len(x_pieces), f...  6.57 us
    pallas_call x4, Pallas kernels, terms(): pl.pallas_call(functools.partial(terms_kernel, layout, split), out_shape=...  5.16 us
    dynamic_slice x3, local copies, waits for them, and re-layouts, ring_gather(): moving = lax.dynamic_slice_in_dim(moving, core * half, half, 0)  3.56 us
    pallas_call x1, Pallas kernels, attend(): pl.pallas_call(functools.partial(attend_kernel, groups), out_shape=jax.Sh...  3.19 us
  transfers between devices with their start and end apart: 39, of which 11 were waited for; matrix products, arithmetic and copies ran while one was open for 10% of the time, Pallas kernels for 13%

commit v1 on v0

--- a/solution.py
+++ b/solution.py
@@ -36,19 +36,31 @@
     return lax.ppermute(value, ("ctx", "zero"), pairs)
 
 
-def ring_gather(shard, core):
-    size = lax.axis_size("ctx")
-    held = [(0, None, shard)]
-    moving = shard
-    half = shard.shape[0] // 2
-    for step in range(1, size // 2 + 1):
-        last = step == size // 2
+class Ring:
+    def __init__(self, shard, core):
+        self.held = [(0, None, shard)]
+        self.moving, self.core, self.at = shard, core, 0
+        self.length = lax.axis_size("ctx") // 2
+
+    def step(self, *after):
+        self.at += 1
+        last = self.at == self.length
         if last:
-            moving = lax.dynamic_slice_in_dim(moving, core * half, half, 0)
-        moving = ring_step(moving)
-        held.append((-step, 0 if last else None, moving))
-        held.append((step, 1 if last else None, swap(moving, "zero", 1)))
-    return held
+            half = self.moving.shape[0] // 2
+            self.moving = lax.dynamic_slice_in_dim(self.moving, self.core * half, half, 0)
+        self.moving = ring_step(tied(self.moving, *after))
+        self.held.append((-self.at, 0 if last else None, self.moving))
+        self.held.append((self.at, 1 if last else None, swap(self.moving, "zero", 1)))
+        return self.moving
+
+    def advance(self, part, parts, *after):
+        while self.at < self.length * (part + 1) // parts:
+            self.step(*after)
+        return self.moving
+
+
+def tied(value, *others):
+    return lax.optimization_barrier((value, *others))[0] if others else value
 
 
 def source_of(steps):
@@ -64,8 +76,50 @@
     return core if share == 0 else 1 - core
 
 
-def project_kernel(layout, pieces, first_call, *refs):
+def token_rows(group, other, size):
+    core = lax.axis_index("zero") % 2
+    if other:
+        core = 1 - core
+    return pl.ds(pl.multiple_of((2 * group + core) * size, 16), size)
+
+
+def deal_kernel(count, *refs):
+    x_refs, outs, sem = refs[:count], refs[count:-1], refs[-1]
+    groups = lax.axis_size("zero") // 2
+    size = x_refs[0].shape[0] // (2 * groups)
+    copies = []
+    for x_ref, out_ref in zip(x_refs, outs):
+        for group in range(groups):
+            copies.append(
+                pltpu.make_async_copy(
+                    x_ref.at[token_rows(group, True, size)],
+                    out_ref.at[pl.ds(group * size, size)],
+                    sem.at[len(copies)],
+                )
+            )
+    for copy in copies:
+        copy.start()
+    for copy in copies:
+        copy.wait()
+
+
+def deal(arrays):
+    tokens, depth = arrays[0].shape
+    part = jax.ShapeDtypeStruct((tokens // 2, depth), arrays[0].dtype)
+    copies = len(arrays) * lax.axis_size("zero") // 2
+    return pl.pallas_call(
+        functools.partial(deal_kernel, len(arrays)),
+        out_shape=[part] * len(arrays),
+        in_specs=[HBM] * len(arrays),
+        out_specs=[HBM] * len(arrays),
+        scratch_shapes=[pltpu.SemaphoreType.DMA((copies,))],
+        compiler_params=pltpu.CompilerParams(vmem_limit_bytes=VMEM_LIMIT),
+    )(*arrays)
+
+
+def project_kernel(layout, first_call, *refs):
     (x_buf, w_buf, x_sem, w_sem) = refs[-4:]
+    pieces, tokens, depth = x_buf.shape
     scale_ref, cos_ref, sin_ref = refs[:3]
     x_refs = refs[3 : 3 + pieces]
     w_refs = refs[3 + pieces : 3 + pieces + len(layout)]
@@ -73,9 +127,20 @@
     zero = lax.axis_index("zero")
     shard_rows = w_refs[0].shape[0]
     x_copies, w_copies = [], []
-    for at, ref in enumerate(x_refs):
-        place = jnp.bitwise_xor(zero, at)
-        x_copies.append(pltpu.make_async_copy(ref, x_buf.at[place], x_sem.at[at]))
+    for m, ref in enumerate(x_refs):
+        target = x_buf.at[jnp.bitwise_xor(zero, m)]
+        if m % 2:
+            x_copies.append(pltpu.make_async_copy(ref, target, x_sem.at[len(x_copies)]))
+            continue
+        size = 2 * tokens // pieces
+        for group in range(pieces // 2):
+            x_copies.append(
+                pltpu.make_async_copy(
+                    ref.at[token_rows(group, False, size)],
+                    target.at[pl.ds(group * size, size)],
+                    x_sem.at[len(x_copies)],
+                )
+            )
     for at, (ref, (steps, share)) in enumerate(zip(w_refs, layout)):
         start = source_of(steps) * shard_rows
         if share is not None:
@@ -86,7 +151,6 @@
         copy.start()
     for copy in x_copies:
         copy.wait()
-    depth = x_buf.shape[2]
     if first_call:
         squares = jnp.zeros((x_buf.shape[1], 128), jnp.float32)
         for at in range(pieces):
@@ -117,21 +181,22 @@
 def project(scale, cos, sin, x_pieces, held, first_call):
     layout = [(steps, share) for steps, share, _ in held]
     shards = [piece for _, _, piece in held]
-    tokens, depth = x_pieces[0].shape
+    tokens, depth = x_pieces[1].shape
+    pieces = len(x_pieces)
     width = shards[0].shape[1]
-    full = depth * len(x_pieces)
+    full = depth * pieces
     out = [jax.ShapeDtypeStruct((tokens, width), jnp.bfloat16)]
     if first_call:
         out.append(jax.ShapeDtypeStruct((tokens, 128), jnp.float32))
     return pl.pallas_call(
-        functools.partial(project_kernel, layout, len(x_pieces), first_call),
+        functools.partial(project_kernel, layout, first_call),
         out_shape=out,
-        in_specs=[VMEM, VMEM, VMEM] + [HBM] * (len(x_pieces) + len(shards)),
+        in_specs=[VMEM] * 3 + [HBM] * (pieces + len(shards)),
         out_specs=[VMEM] * len(out),
         scratch_shapes=[
-            pltpu.VMEM((len(x_pieces), tokens, depth), jnp.bfloat16),
+            pltpu.VMEM((pieces, tokens, depth), jnp.bfloat16),
             pltpu.VMEM((full, width), jnp.bfloat16),
-            pltpu.SemaphoreType.DMA((len(x_pieces),)),
+            pltpu.SemaphoreType.DMA((pieces // 2 * (1 + pieces // 2),)),
             pltpu.SemaphoreType.DMA((len(shards),)),
         ],
         compiler_params=pltpu.CompilerParams(vmem_limit_bytes=VMEM_LIMIT),
@@ -301,13 +366,10 @@
     )(*keeps, *gots)
 
 
-def broadcast_from(value, root):
-    me = lax.axis_index("ctx")
-    for bit in range(int(math.log2(lax.axis_size("ctx")))):
-        other = swap(value, "ctx", 1 << bit)
-        same = ((me >> bit) & 1) == ((root >> bit) & 1)
-        value = jnp.where(same, value, other)
-    return value
+def exchange_from(value, root, bit):
+    other = swap(value, "ctx", 1 << bit)
+    same = ((lax.axis_index("ctx") >> bit) & 1) == ((root >> bit) & 1)
+    return jnp.where(same, value, other)
 
 
 def local(
@@ -328,12 +390,12 @@
     groups = zero_size // 2
     size = tokens // zero_size
 
-    by_core = activations.reshape(groups, 2, size, depth)
-    mine = lax.dynamic_index_in_dim(by_core, core, 1, keepdims=False).reshape(-1, depth)
-    theirs = lax.dynamic_index_in_dim(by_core, 1 - core, 1, keepdims=False).reshape(-1, depth)
-    x_pieces = [mine] + [
-        swap(theirs if m % 2 else mine, "zero", m) for m in range(1, zero_size)
-    ]
+    blocks = {0: activations}
+    stride = groups
+    while stride > 1:
+        for known in range(0, zero_size, 2 * stride):
+            blocks[known + stride] = swap(blocks[known], "zero", stride)
+        stride //= 2
 
     shard_rows = kv_weight.shape[0]
     gain = lax.dynamic_slice_in_dim(norm_gain, ctx_rank * shard_rows, shard_rows)
@@ -350,9 +412,25 @@
     kv_pair = (of_chip(kv_weight[:, 0, :], 1).astype(jnp.float32) * gain).astype(jnp.bfloat16)
     query_pair = (of_chip(query_weight, 1).astype(jnp.float32) * gain).astype(jnp.bfloat16)
     out_pair = of_chip(out_weight, 0)
-    kv_held = ring_gather(kv_pair, core)
-    query_held = ring_gather(query_pair, core)
-    out_held = ring_gather(out_pair, core)
+    kv_ring = Ring(kv_pair, core)
+    query_ring = Ring(query_pair, core)
+    out_ring = Ring(out_pair, core)
+    kv_ring.advance(0, 4)
+    query_ring.advance(0, 4)
+    kv_ring.advance(1, 4)
+    third = kv_ring.advance(2, 4)
+    second = query_ring.advance(1, 4, third)
+    done = kv_ring.advance(3, 4)
+    query_ring.advance(2, 4, done)
+    query_ring.advance(3, 4)
+    out_ring.advance(0, 4, query_ring.moving)
+
+    for known in range(2, zero_size, 2):
+        blocks[known] = tied(blocks[known], third)
+    own = deal([blocks[0]]) + (deal([blocks[m] for m in range(2, zero_size, 2)]))
+    x_pieces = []
+    for m, theirs in zip(range(0, zero_size, 2), own):
+        x_pieces += [blocks[m], swap(theirs, "zero", 1)]
 
     half = head // 2
     frequency = jnp.power(
@@ -367,27 +445,37 @@
     sin = jnp.concatenate([-sin_half, sin_half], -1)
     shrink = head ** (-0.5)
 
-    near, scale = project(cos, cos, sin, x_pieces, kv_held, True)
+    near, scale = project(cos, cos, sin, x_pieces, kv_ring.held, True)
+    (queries,) = project(
+        scale, cos * shrink, sin * shrink, x_pieces, query_ring.held, False
+    )
     anchor = anchor_index[0]
-    far = broadcast_from(near, anchor)
+    far = near
+    bits = int(math.log2(ctx_size))
+    for bit in range(bits):
+        far = exchange_from(tied(far, queries) if bit == bits - 1 else far, anchor, bit)
+        if bit == bits - 2:
+            out_ring.advance(1, 4, far)
     near_other = swap(near, "zero", 1)
     far_other = swap(far, "zero", 1)
-    (queries,) = project(scale, cos * shrink, sin * shrink, x_pieces, query_held, False)
+    out_ring.advance(2, 4, far)
+    out_ring.advance(3, 4)
     far_mask = jnp.where(ctx_rank != anchor, anchor_mask[0], 0)
     attended = attend(groups, tile_mask[0], far_mask, queries, near, near_other, far, far_other)
 
     slots = []
-    for steps, share, piece in out_held:
+    for steps, share, piece in out_ring.held:
         if share == 1:
             slots[-1][1].append((share, piece))
         else:
             slots.append((steps, [(share, piece)]))
     per = max(1, ctx_size // CHUNKS)
+    cuts = [0] + list(range(per + 1, ctx_size, per)) + [ctx_size]
     step_groups, keeps, gots = [], [], []
     top = zero_size // 2
-    for at in range(0, ctx_size, per):
-        step_groups.append([steps for steps, _ in slots[at : at + per]])
-        keep, send = terms(top, attended, [pieces for _, pieces in slots[at : at + per]])
+    for first, end in zip(cuts, cuts[1:]):
+        step_groups.append([steps for steps, _ in slots[first:end]])
+        keep, send = terms(top, attended, [pieces for _, pieces in slots[first:end]])
         got = swap(send, "zero", top)
         stride = top // 2
         while stride > 1:

time: 120 us -> 129 us (1.075)
  waiting for transfers between devices: 55.4 us -> 65.8 us
  local copies, waits for them, and re-layouts: 7.02 us -> 3.93 us
  other arithmetic: 6.06 us -> 7.62 us
    ppermute x12, waiting for transfers between devices: 17.3 us -> 31.9 us  [ring_step(): return lax.ppermute(value, ('ctx', 'zero'), pairs)]
    ppermute x27, waiting for transfers between devices: 38.1 us -> 33.9 us  [swap(): return lax.ppermute(value, axis, pairs)]
    dynamic_slice x4 -> x3, local copies, waits for them, and re-layouts: 5.69 us -> 1.77 us  [step(): lax.dynamic_slice_in_dim(self.moving, self.core * half, half, 0)]
    pallas_call x4, Pallas kernels: 5.16 us -> 3.18 us  [terms(): pl.pallas_call(functools.partial(terms_kernel, layout, split), out_shape=...]
    ppermute x27, starting transfers between devices: 12.5 us -> 13.9 us  [swap(): return lax.ppermute(value, axis, pairs)]
    pallas_call x2 -> x4, Pallas kernels: 6.57 us -> 7.4 us  [the longest x2 6.52 us: project(): pl.pallas_call(functools.partial(project_kernel, layout, first_call), out...]
  transfers between devices with their start and end apart: 39 -> 39, of which waited for: 11 -> 15; matrix products, arithmetic and copies ran while one was open for 10% -> 7% of each run, Pallas kernels for 13% -> 11%
where the time goes in v1:
time: 129 us; the launch traced here: 128 us
  waiting for transfers between devices  65.8 us (51%)
  starting transfers between devices  34.9 us (27%)
  Pallas kernels  14.9 us (12%)
  other arithmetic  7.62 us (6%)
  local copies, waits for them, and re-layouts  3.93 us (3%)
    ppermute x27, waiting for transfers between devices, swap(): return lax.ppermute(value, axis, pairs)  33.9 us
    ppermute x12, waiting for transfers between devices, ring_step(): return lax.ppermute(value, ('ctx', 'zero'), pairs)  31.9 us
    ppermute x12, starting transfers between devices, ring_step(): return lax.ppermute(value, ('ctx', 'zero'), pairs)  21.1 us
    ppermute x27, starting transfers between devices, swap(): return lax.ppermute(value, axis, pairs)  13.9 us
    pallas_call x2, Pallas kernels, project(): pl.pallas_call(functools.partial(project_kernel, layout, first_call), out...  6.52 us
    pallas_call x1, Pallas kernels, attend(): pl.pallas_call(functools.partial(attend_kernel, groups), out_shape=jax.Sh...  3.18 us
    pallas_call x4, Pallas kernels, terms(): pl.pallas_call(functools.partial(terms_kernel, layout, split), out_shape=...  3.18 us
  transfers between devices with their start and end apart: 39, of which 15 were waited for; matrix products, arithmetic and copies ran while one was open for 7% of the time, Pallas kernels for 11%

profile of v1, /device:TPU:0, one launch (start us, length us, event | category | flops | bytes accessed | tf_op | source)
XLA Modules:
  0.0 128.3 jit_solution(16721266456235782320)
XLA Ops:
  0.5 0.8 dynamic-slice_convert_fusion
  1.7 1.1 multiply_convert_fusion.1.refs_7_
  2.8 3.0 %collective-permute-start.3 = (bf16[512,256]{1,0:T(8,128)(2,1)S(1)}, bf16[512,256]{1,0:T(8,128)(2,1)S(1)}, u32[]{:S(2)}, u32[]{:S(2)}) collective-permute-start(bf16[512,256]{1,0:T(8,128)(2,1)S(1)} %multiply_convert_fusion.1.refs_7_), channel_id=1, source_target_pairs={{0,8},{1,5},{2,10},{3,7},{8,16},{9,1},{10,18},{11,3},{16,24},{17,9... | collective-permute-start | bytes 786440 | tf_op jit(solution)/shard_map/ppermute | solution.py:36
  5.8 1.2 multiply_convert_fusion.refs_7_
  7.0 3.1 %collective-permute-done.3.refs_8_ = bf16[512,256]{1,0:T(8,128)(2,1)S(1)} collective-permute-done((bf16[512,256]{1,0:T(8,128)(2,1)S(1)}, bf16[512,256]{1,0:T(8,128)(2,1)S(1)}, u32[]{:S(2)}, u32[]{:S(2)}) %collective-permute-start.3) | collective-permute-done | bytes 262176 | tf_op jit(solution)/shard_map/ppermute | solution.py:36
  10.0 2.1 %collective-permute-start.4 = (bf16[512,256]{1,0:T(8,128)(2,1)S(1)}, bf16[512,256]{1,0:T(8,128)(2,1)S(1)}, u32[]{:S(2)}, u32[]{:S(2)}) collective-permute-start(bf16[512,256]{1,0:T(8,128)(2,1)S(1)} %collective-permute-done.3.refs_8_), channel_id=1, source_target_pairs={{0,8},{1,5},{2,10},{3,7},{8,16},{9,1},{10,18},{11,3},{16,24},{17,9... | collective-permute-start | bytes 786440 | tf_op jit(solution)/shard_map/ppermute | solution.py:36
  12.1 1.6 %collective-permute-start.13 = (bf16[512,512]{1,0:T(8,128)(2,1)S(1)}, bf16[512,512]{1,0:T(8,128)(2,1)}, u32[]{:S(2)}, u32[]{:S(2)}) collective-permute-start(bf16[512,512]{1,0:T(8,128)(2,1)S(1)} %multiply_convert_fusion.refs_7_), channel_id=1, source_target_pairs={{0,8},{1,5},{2,10},{3,7},{8,16},{9,1},{10,18},{11,3},{16,24},{17,9... | collective-permute-start | bytes 1572872 | tf_op jit(solution)/shard_map/ppermute | solution.py:36
  13.7 1.5 %collective-permute-start.1 = (bf16[512,1024]{1,0:T(8,128)(2,1)S(1)}, bf16[512,1024]{1,0:T(8,128)(2,1)S(1)}, u32[]{:S(2)}, u32[]{:S(2)}) collective-permute-start(bf16[512,1024]{1,0:T(8,128)(2,1)S(1)} %copy-done), channel_id=1, source_target_pairs={{0,2},{1,3},{2,0},{3,1},{4,6},{5,7},{6,4},{7,5},{8,10},{9,11},{10,... | collective-permute-start | bytes 3145736 | tf_op jit(solution)/shard_map/ppermute | solution.py:21
  15.2 1.2 collective-permute-done.4.refs_10_
  16.4 2.1 %collective-permute-start.5 = (bf16[512,256]{1,0:T(8,128)(2,1)S(1)}, bf16[512,256]{1,0:T(8,128)(2,1)}, u32[]{:S(2)}, u32[]{:S(2)}) collective-permute-start(bf16[512,256]{1,0:T(8,128)(2,1)S(1)} %collective-permute-done.4.refs_10_), channel_id=1, source_target_pairs={{0,8},{1,5},{2,10},{3,7},{8,16},{9,1},{10,18},{11,3},{16,24},{17,9... | collective-permute-start | bytes 786440 | tf_op jit(solution)/shard_map/ppermute | solution.py:36
  18.5 3.6 %collective-permute-done.13.refs_8_ = bf16[512,512]{1,0:T(8,128)(2,1)} collective-permute-done((bf16[512,512]{1,0:T(8,128)(2,1)S(1)}, bf16[512,512]{1,0:T(8,128)(2,1)}, u32[]{:S(2)}, u32[]{:S(2)}) %collective-permute-start.13) | collective-permute-done | bytes 524320 | tf_op jit(solution)/shard_map/ppermute | solution.py:36
  22.1 2.8 %collective-permute-done.5.refs_12_ = bf16[512,256]{1,0:T(8,128)(2,1)} collective-permute-done((bf16[512,256]{1,0:T(8,128)(2,1)S(1)}, bf16[512,256]{1,0:T(8,128)(2,1)}, u32[]{:S(2)}, u32[]{:S(2)}) %collective-permute-start.5) | collective-permute-done | bytes 262176 | tf_op jit(solution)/shard_map/ppermute | solution.py:36
  24.9 2.1 %collective-permute-start.15 = (bf16[512,512]{1,0:T(8,128)(2,1)}, bf16[512,512]{1,0:T(8,128)(2,1)}, u32[]{:S(2)}, u32[]{:S(2)}) collective-permute-start(bf16[512,512]{1,0:T(8,128)(2,1)} %collective-permute-done.13.refs_8_), channel_id=1, source_target_pairs={{0,8},{1,5},{2,10},{3,7},{8,16},{9,1},{10,18},{11,3},{16,24},{17,9... | collective-permute-start | bytes 1572872 | tf_op jit(solution)/shard_map/ppermute | solution.py:36
  27.0 0.8 shard_map.82
  28.0 1.0 constant_dynamic-slice_fusion.2
  28.9 1.6 %collective-permute-start.10 = (bf16[256,256]{1,0:T(8,128)(2,1)S(1)}, bf16[256,256]{1,0:T(8,128)(2,1)S(1)}, u32[]{:S(2)}, u32[]{:S(2)}) collective-permute-start(bf16[256,256]{1,0:T(8,128)(2,1)S(1)} %constant_dynamic-slice_fusion.2), channel_id=1, source_target_pairs={{0,8},{1,5},{2,10},{3,7},{8,16},{9,1},{10,18},{11,3},{16,24},{17,9... | collective-permute-start | bytes 393224 | tf_op jit(solution)/shard_map/ppermute | solution.py:36
  30.6 5.2 %collective-permute-done.10.refs_14_ = bf16[256,256]{1,0:T(8,128)(2,1)S(1)} collective-permute-done((bf16[256,256]{1,0:T(8,128)(2,1)S(1)}, bf16[256,256]{1,0:T(8,128)(2,1)S(1)}, u32[]{:S(2)}, u32[]{:S(2)}) %collective-permute-start.10) | collective-permute-done | bytes 131104 | tf_op jit(solution)/shard_map/ppermute | solution.py:36
  35.7 2.1 %collective-permute-start.17 = (bf16[512,512]{1,0:T(8,128)(2,1)}, bf16[512,512]{1,0:T(8,128)(2,1)S(1)}, u32[]{:S(2)}, u32[]{:S(2)}) collective-permute-start(bf16[512,512]{1,0:T(8,128)(2,1)} %collective-permute-done.15.refs_10_), channel_id=1, source_target_pairs={{0,8},{1,5},{2,10},{3,7},{8,16},{9,1},{10,18},{11,3},{16,24},{17,9... | collective-permute-start | bytes 1572872 | tf_op jit(solution)/shard_map/ppermute | solution.py:36
  40.0 5.2 %collective-permute-done.17.refs_12_ = bf16[512,512]{1,0:T(8,128)(2,1)S(1)} collective-permute-done((bf16[512,512]{1,0:T(8,128)(2,1)}, bf16[512,512]{1,0:T(8,128)(2,1)S(1)}, u32[]{:S(2)}, u32[]{:S(2)}) %collective-permute-start.17) | collective-permute-done | bytes 524320 | tf_op jit(solution)/shard_map/ppermute | solution.py:36
  45.1 0.8 constant_dynamic-slice_fusion.1
  45.9 2.1 %collective-permute-start.19 = (bf16[256,512]{1,0:T(8,128)(2,1)}, bf16[256,512]{1,0:T(8,128)(2,1)}, u32[]{:S(2)}, u32[]{:S(2)}) collective-permute-start(bf16[256,512]{1,0:T(8,128)(2,1)} %constant_dynamic-slice_fusion.1), channel_id=1, source_target_pairs={{0,8},{1,5},{2,10},{3,7},{8,16},{9,1},{10,18},{11,3},{16,24},{17,9... | collective-permute-start | bytes 786440 | tf_op jit(solution)/shard_map/ppermute | solution.py:36
  48.0 0.8 broadcast_multiply_fusion
  48.9 2.8 %shard_map.84 = (bf16[256,256]{1,0:T(8,128)(2,1)}, f32[256,128]{1,0:T(8,128)S(1)}) custom-call(f32[256,128]{1,0:T(8,128)S(1)} %get-tuple-element.46.refs_0_.refs_1_, f32[256,128]{1,0:T(8,128)S(1)} %get-tuple-element.46.refs_0_.refs_1_, f32[256,128]{1,0:T(8,128)S(1)} %get-tuple-element.40.refs_2_, bf16[512,1024]{1,0:T(8,128)(2,1)S(1)} %copy-done, ...), custom_call_target="tpu_custom_call" | custom-call | flops 536870912 | bytes 4194304 | tf_op jit(solution)/shard_map/pallas_call | solution.py:191
  51.7 0.6 copy-done.13
  53.0 1.4 %maximum_select_fusion.1.refs_0_ = bf16[512,512]{1,0:T(8,128)(2,1)S(1)} fusion(bf16[256,512]{1,0:T(8,128)(2,1)} %collective-permute-done.26, bf16[256,512]{1,0:T(8,128)(2,1)} %param.12, pred[]{:T(512)S(6)} %eq.18), kind=kLoop, calls=%fused_computation.2 | loop fusion | flops 2359296 | bytes 1048577 | tf_op jit(solution)/shard_map/jit(_where)/select_n | solution.py:406
  54.4 1.4 %collective-permute-start.14 = (bf16[512,512]{1,0:T(8,128)(2,1)}, bf16[512,512]{1,0:T(8,128)(2,1)}, u32[]{:S(2)}, u32[]{:S(2)}) collective-permute-start(bf16[512,512]{1,0:T(8,128)(2,1)} %collective-permute-done.13.refs_8_), channel_id=1, source_target_pairs={{0,1},{1,0},{2,3},{3,2},{4,5},{5,4},{6,7},{7,6},{8,9},{9,8},{10,11... | collective-permute-start | bytes 1572872 | tf_op jit(solution)/shard_map/ppermute | solution.py:21
  56.4 1.6 %collective-permute-start.27 = (bf16[512,512]{1,0:T(8,128)(2,1)S(1)}, bf16[512,512]{1,0:T(8,128)(2,1)S(1)}, u32[]{:S(2)}, u32[]{:S(2)}) collective-permute-start(bf16[512,512]{1,0:T(8,128)(2,1)S(1)} %maximum_select_fusion.1.refs_0_), channel_id=1, source_target_pairs={{0,8},{1,5},{2,10},{3,7},{8,16},{9,1},{10,18},{11,3},{16,24},{17,9... | collective-permute-start | bytes 1572872 | tf_op jit(solution)/shard_map/ppermute | solution.py:36
  58.0 0.9 broadcast_select_fusion
  59.0 1.6 %collective-permute-start.23 = (bf16[256,256]{1,0:T(8,128)(2,1)S(1)}, bf16[256,256]{1,0:T(8,128)(2,1)}, u32[]{:S(2)}, u32[]{:S(2)}) collective-permute-start(bf16[256,256]{1,0:T(8,128)(2,1)S(1)} %broadcast_select_fusion), channel_id=1, source_target_pairs={{0,8},{4,12},{8,0},{12,4},{16,24},{20,28},{24,16},{28,20},{1,9},{5... | collective-permute-start | bytes 393224 | tf_op jit(solution)/shard_map/ppermute | solution.py:21
  60.5 6.9 %collective-permute-done.23 = bf16[256,256]{1,0:T(8,128)(2,1)} collective-permute-done((bf16[256,256]{1,0:T(8,128)(2,1)S(1)}, bf16[256,256]{1,0:T(8,128)(2,1)}, u32[]{:S(2)}, u32[]{:S(2)}) %collective-permute-start.23) | collective-permute-done | bytes 131104 | tf_op jit(solution)/shard_map/ppermute | solution.py:21
  67.5 0.9 broadcast_select_fusion.1
  68.4 2.6 %collective-permute-start.29 = (bf16[512,512]{1,0:T(8,128)(2,1)S(1)}, bf16[512,512]{1,0:T(8,128)(2,1)}, u32[]{:S(2)}, u32[]{:S(2)}) collective-permute-start(bf16[512,512]{1,0:T(8,128)(2,1)S(1)} %collective-permute-done.27.refs_1_), channel_id=1, source_target_pairs={{0,8},{1,5},{2,10},{3,7},{8,16},{9,1},{10,18},{11,3},{16,24},{17,9... | collective-permute-start | bytes 1572872 | tf_op jit(solution)/shard_map/ppermute | solution.py:36
  71.1 3.7 %shard_map.85.q_ref = bf16[256,512]{1,0:T(8,128)(2,1)S(1)} custom-call(f32[256,128]{1,0:T(8,128)S(1)} %copy-done.14, f32[256,128]{1,0:T(8,128)S(1)} %copy-done.6, f32[256,128]{1,0:T(8,128)S(1)} %get-tuple-element.39.refs_2_, bf16[512,1024]{1,0:T(8,128)(2,1)} %refs_3_.3, bf16[256,1024]{1,0:T(8,128)(2,1)S(1)} %collective-permute-done.refs_4_, ...), custom_call_target="tpu_custom_call" | custom-call | flops 1073741824 | bytes 6291456 | tf_op jit(solution)/shard_map/pallas_call | solution.py:191
  74.8 0.7 copy-done.11
  75.5 1.7 %collective-permute-start.24 = (bf16[256,256]{1,0:T(8,128)(2,1)S(1)}, bf16[256,256]{1,0:T(8,128)(2,1)S(1)}, u32[]{:S(2)}, u32[]{:S(2)}) collective-permute-start(bf16[256,256]{1,0:T(8,128)(2,1)S(1)} %broadcast_select_fusion.1), channel_id=1, source_target_pairs={{0,16},{4,20},{8,24},{12,28},{16,0},{20,4},{24,8},{28,12},{1,17},{... | collective-permute-start | bytes 393224 | tf_op jit(solution)/shard_map/ppermute | solution.py:21
  77.2 7.6 %collective-permute-done.24 = bf16[256,256]{1,0:T(8,128)(2,1)S(1)} collective-permute-done((bf16[256,256]{1,0:T(8,128)(2,1)S(1)}, bf16[256,256]{1,0:T(8,128)(2,1)S(1)}, u32[]{:S(2)}, u32[]{:S(2)}) %collective-permute-start.24) | collective-permute-done | bytes 131104 | tf_op jit(solution)/shard_map/ppermute | solution.py:21
  86.0 8.3 %collective-permute-done.31.refs_0_ = bf16[512,512]{1,0:T(8,128)(2,1)S(1)} collective-permute-done((bf16[512,512]{1,0:T(8,128)(2,1)}, bf16[512,512]{1,0:T(8,128)(2,1)S(1)}, u32[]{:S(2)}, u32[]{:S(2)}) %collective-permute-start.31) | collective-permute-done | bytes 524320 | tf_op jit(solution)/shard_map/ppermute | solution.py:36
  95.0 3.2 %shard_map.86.a_ref = bf16[256,512]{1,0:T(8,128)(2,1)S(1)} custom-call(s32[4,4]{1,0:T(4,128)S(1)} %bitcast.9, s32[4,4]{1,0:T(4,128)S(1)} %select_bitcast_fusion.far_ref, bf16[256,512]{1,0:T(8,128)(2,1)S(1)} %copy-done.12, bf16[256,256]{1,0:T(8,128)(2,1)} %get-tuple-element.26.near0, bf16[256,256]{1,0:T(8,128)(2,1)S(1)} %collective-permute-done.21.near1, ...), custom_call_target="tpu_custom_call" | custom-call | flops 536870912 | bytes 1048576 | tf_op jit(solution)/shard_map/pallas_call | solution.py:275
  98.2 2.6 %collective-permute-done.33.refs_0_ = bf16[256,512]{1,0:T(8,128)(2,1)S(1)} collective-permute-done((bf16[256,512]{1,0:T(8,128)(2,1)S(1)}, bf16[256,512]{1,0:T(8,128)(2,1)S(1)}, u32[]{:S(2)}, u32[]{:S(2)}) %collective-permute-start.33) | collective-permute-done | bytes 262176 | tf_op jit(solution)/shard_map/ppermute | solution.py:36
  100.8 0.7 shard_map.87
  101.5 1.6 %collective-permute-start.35 = (bf16[128,1536]{1,0:T(8,128)(2,1)S(1)}, bf16[128,1536]{1,0:T(8,128)(2,1)S(1)}, u32[]{:S(2)}, u32[]{:S(2)}) collective-permute-start(bf16[128,1536]{1,0:T(8,128)(2,1)S(1)} %get-tuple-element.35), channel_id=1, source_target_pairs={{0,2},{1,3},{2,0},{3,1},{4,6},{5,7},{6,4},{7,5},{8,10},{9,11},{10,... | collective-permute-start | bytes 1179656 | tf_op jit(solution)/shard_map/ppermute | solution.py:21
  103.1 1.5 %shard_map.88 = (f32[128,1024]{1,0:T(8,128)S(1)}, bf16[128,1024]{1,0:T(8,128)(2,1)S(1)}) custom-call(bf16[256,512]{1,0:T(8,128)(2,1)S(1)} %shard_map.86.a_ref, bf16[512,512]{1,0:T(8,128)(2,1)} %collective-permute-done.29.refs_0_, bf16[512,512]{1,0:T(8,128)(2,1)S(1)} %collective-permute-done.30.refs_1_), custom_call_target="tpu_custom_call" | custom-call | flops 268435456 | bytes 2097152 | tf_op jit(solution)/shard_map/pallas_call | solution.py:321
  105.7 1.6 %collective-permute-start.37 = (bf16[128,1024]{1,0:T(8,128)(2,1)S(1)}, bf16[128,1024]{1,0:T(8,128)(2,1)S(1)}, u32[]{:S(2)}, u32[]{:S(2)}) collective-permute-start(bf16[128,1024]{1,0:T(8,128)(2,1)S(1)} %get-tuple-element.37), channel_id=1, source_target_pairs={{0,2},{1,3},{2,0},{3,1},{4,6},{5,7},{6,4},{7,5},{8,10},{9,11},{10,... | collective-permute-start | bytes 786440 | tf_op jit(solution)/shard_map/ppermute | solution.py:21
  107.7 0.6 collective-permute-start.38
  108.3 5.2 %collective-permute-done.35.refs_4_ = bf16[128,1536]{1,0:T(8,128)(2,1)S(1)} collective-permute-done((bf16[128,1536]{1,0:T(8,128)(2,1)S(1)}, bf16[128,1536]{1,0:T(8,128)(2,1)S(1)}, u32[]{:S(2)}, u32[]{:S(2)}) %collective-permute-start.35) | collective-permute-done | bytes 393248 | tf_op jit(solution)/shard_map/ppermute | solution.py:21
  113.5 5.6 %collective-permute-done.36.refs_5_ = bf16[128,1024]{1,0:T(8,128)(2,1)S(1)} collective-permute-done((bf16[128,1024]{1,0:T(8,128)(2,1)S(1)}, bf16[128,1024]{1,0:T(8,128)(2,1)S(1)}, u32[]{:S(2)}, u32[]{:S(2)}) %collective-permute-start.36) | collective-permute-done | bytes 262176 | tf_op jit(solution)/shard_map/ppermute | solution.py:21
  119.1 8.0 %collective-permute-done.38.refs_7_ = bf16[128,512]{1,0:T(8,128)(2,1)S(1)} collective-permute-done((bf16[128,512]{1,0:T(8,128)(2,1)S(1)}, bf16[128,512]{1,0:T(8,128)(2,1)S(1)}, u32[]{:S(2)}, u32[]{:S(2)}) %collective-permute-start.38) | collective-permute-done | bytes 131104 | tf_op jit(solution)/shard_map/ppermute | solution.py:21
  127.1 1.1 shard_map.91
  (91 shorter events, 7.0 us)
Async XLA Ops:
  0.0 13.7 %copy-start = (bf16[512,1024]{1,0:T(8,128)(2,1)S(1)}, bf16[512,1024]{1,0:T(8,128)(2,1)}, u32[]{:S(2)}) copy-start(bf16[512,1024]{1,0:T(8,128)(2,1)} %refs_3_.3) | copy-start | bytes 3145732
  0.0 1.6 %collective-permute-start.2 = (bf16[512,128]{1,0:T(8,128)(2,1)}, bf16[512,128]{1,0:T(8,128)(2,1)S(1)}, u32[]{:S(2)}, u32[]{:S(2)}) collective-permute-start(bf16[512,128]{1,0:T(8,128)(2,1)} %bitcast.10), channel_id=1, source_target_pairs={{0,1},{1,0},{2,3},{3,2},{4,5},{5,4},{6,7},{7,6},{8,9},{9,8},{10,11... | collective-permute-start | bytes 393224 | tf_op jit(solution)/shard_map/ppermute | solution.py:21
  0.5 5.3 %collective-permute-start.12 = (bf16[512,256]{1,0:T(8,128)(2,1)}, bf16[512,256]{1,0:T(8,128)(2,1)S(1)}, u32[]{:S(2)}, u32[]{:S(2)}) collective-permute-start(bf16[512,256]{1,0:T(8,128)(2,1)} %param.10), channel_id=1, source_target_pairs={{0,1},{1,0},{2,3},{3,2},{4,5},{5,4},{6,7},{7,6},{8,9},{9,8},{10,11... | collective-permute-start | bytes 786440 | tf_op jit(solution)/shard_map/ppermute | solution.py:21
  2.8 7.3 %collective-permute-start.3 = (bf16[512,256]{1,0:T(8,128)(2,1)S(1)}, bf16[512,256]{1,0:T(8,128)(2,1)S(1)}, u32[]{:S(2)}, u32[]{:S(2)}) collective-permute-start(bf16[512,256]{1,0:T(8,128)(2,1)S(1)} %multiply_convert_fusion.1.refs_7_), channel_id=1, source_target_pairs={{0,8},{1,5},{2,10},{3,7},{8,16},{9,1},{10,18},{11,3},{16,24},{17,9... | collective-permute-start | bytes 786440 | tf_op jit(solution)/shard_map/ppermute | solution.py:36
  10.0 12.1 %copy-start.7 = (bf16[512,256]{1,0:T(8,128)(2,1)}, bf16[512,256]{1,0:T(8,128)(2,1)S(1)}, u32[]{:S(2)}) copy-start(bf16[512,256]{1,0:T(8,128)(2,1)S(1)} %collective-permute-done.3.refs_8_) | copy-start | bytes 786436
  10.0 6.4 %collective-permute-start.4 = (bf16[512,256]{1,0:T(8,128)(2,1)S(1)}, bf16[512,256]{1,0:T(8,128)(2,1)S(1)}, u32[]{:S(2)}, u32[]{:S(2)}) collective-permute-start(bf16[512,256]{1,0:T(8,128)(2,1)S(1)} %collective-permute-done.3.refs_8_), channel_id=1, source_target_pairs={{0,8},{1,5},{2,10},{3,7},{8,16},{9,1},{10,18},{11,3},{16,24},{17,9... | collective-permute-start | bytes 786440 | tf_op jit(solution)/shard_map/ppermute | solution.py:36
  12.1 10.0 %collective-permute-start.13 = (bf16[512,512]{1,0:T(8,128)(2,1)S(1)}, bf16[512,512]{1,0:T(8,128)(2,1)}, u32[]{:S(2)}, u32[]{:S(2)}) collective-permute-start(bf16[512,512]{1,0:T(8,128)(2,1)S(1)} %multiply_convert_fusion.refs_7_), channel_id=1, source_target_pairs={{0,8},{1,5},{2,10},{3,7},{8,16},{9,1},{10,18},{11,3},{16,24},{17,9... | collective-permute-start | bytes 1572872 | tf_op jit(solution)/shard_map/ppermute | solution.py:36
  13.7 24.2 %collective-permute-start.1 = (bf16[512,1024]{1,0:T(8,128)(2,1)S(1)}, bf16[512,1024]{1,0:T(8,128)(2,1)S(1)}, u32[]{:S(2)}, u32[]{:S(2)}) collective-permute-start(bf16[512,1024]{1,0:T(8,128)(2,1)S(1)} %copy-done), channel_id=1, source_target_pairs={{0,2},{1,3},{2,0},{3,1},{4,6},{5,7},{6,4},{7,5},{8,10},{9,11},{10,... | collective-permute-start | bytes 3145736 | tf_op jit(solution)/shard_map/ppermute | solution.py:21
  16.4 8.5 %collective-permute-start.5 = (bf16[512,256]{1,0:T(8,128)(2,1)S(1)}, bf16[512,256]{1,0:T(8,128)(2,1)}, u32[]{:S(2)}, u32[]{:S(2)}) collective-permute-start(bf16[512,256]{1,0:T(8,128)(2,1)S(1)} %collective-permute-done.4.refs_10_), channel_id=1, source_target_pairs={{0,8},{1,5},{2,10},{3,7},{8,16},{9,1},{10,18},{11,3},{16,24},{17,9... | collective-permute-start | bytes 786440 | tf_op jit(solution)/shard_map/ppermute | solution.py:36
  24.9 10.8 %collective-permute-start.15 = (bf16[512,512]{1,0:T(8,128)(2,1)}, bf16[512,512]{1,0:T(8,128)(2,1)}, u32[]{:S(2)}, u32[]{:S(2)}) collective-permute-start(bf16[512,512]{1,0:T(8,128)(2,1)} %collective-permute-done.13.refs_8_), channel_id=1, source_target_pairs={{0,8},{1,5},{2,10},{3,7},{8,16},{9,1},{10,18},{11,3},{16,24},{17,9... | collective-permute-start | bytes 1572872 | tf_op jit(solution)/shard_map/ppermute | solution.py:36
  27.9 10.9 %collective-permute-start = (bf16[256,1024]{1,0:T(8,128)(2,1)}, bf16[256,1024]{1,0:T(8,128)(2,1)S(1)}, u32[]{:S(2)}, u32[]{:S(2)}) collective-permute-start(bf16[256,1024]{1,0:T(8,128)(2,1)} %shard_map.82), channel_id=1, source_target_pairs={{0,1},{1,0},{2,3},{3,2},{4,5},{5,4},{6,7},{7,6},{8,9},{9,8},{10,11... | collective-permute-start | bytes 1572872 | tf_op jit(solution)/shard_map/ppermute | solution.py:21
  27.9 9.9 %copy-start.8 = (bf16[512,256]{1,0:T(8,128)(2,1)S(1)}, bf16[512,256]{1,0:T(8,128)(2,1)}, u32[]{:S(2)}) copy-start(bf16[512,256]{1,0:T(8,128)(2,1)} %copy-done.7) | copy-start | bytes 786436
  28.9 6.8 %collective-permute-start.10 = (bf16[256,256]{1,0:T(8,128)(2,1)S(1)}, bf16[256,256]{1,0:T(8,128)(2,1)S(1)}, u32[]{:S(2)}, u32[]{:S(2)}) collective-permute-start(bf16[256,256]{1,0:T(8,128)(2,1)S(1)} %constant_dynamic-slice_fusion.2), channel_id=1, source_target_pairs={{0,8},{1,5},{2,10},{3,7},{8,16},{9,1},{10,18},{11,3},{16,24},{17,9... | collective-permute-start | bytes 393224 | tf_op jit(solution)/shard_map/ppermute | solution.py:36
  35.7 9.4 %collective-permute-start.17 = (bf16[512,512]{1,0:T(8,128)(2,1)}, bf16[512,512]{1,0:T(8,128)(2,1)S(1)}, u32[]{:S(2)}, u32[]{:S(2)}) collective-permute-start(bf16[512,512]{1,0:T(8,128)(2,1)} %collective-permute-done.15.refs_10_), channel_id=1, source_target_pairs={{0,8},{1,5},{2,10},{3,7},{8,16},{9,1},{10,18},{11,3},{16,24},{17,9... | collective-permute-start | bytes 1572872 | tf_op jit(solution)/shard_map/ppermute | solution.py:36
  37.9 2.0 %collective-permute-start.7 = (bf16[512,256]{1,0:T(8,128)(2,1)S(1)}, bf16[512,256]{1,0:T(8,128)(2,1)S(1)}, u32[]{:S(2)}, u32[]{:S(2)}) collective-permute-start(bf16[512,256]{1,0:T(8,128)(2,1)S(1)} %copy-done.8), channel_id=1, source_target_pairs={{0,1},{1,0},{2,3},{3,2},{4,5},{5,4},{6,7},{7,6},{8,9},{9,8},{10,11... | collective-permute-start | bytes 786440 | tf_op jit(solution)/shard_map/ppermute | solution.py:21
  38.0 10.9 %copy-start.1 = (bf16[512,1024]{1,0:T(8,128)(2,1)}, bf16[512,1024]{1,0:T(8,128)(2,1)S(1)}, u32[]{:S(2)}) copy-start(bf16[512,1024]{1,0:T(8,128)(2,1)S(1)} %collective-permute-done.1.refs_0_.refs_5_) | copy-start | bytes 3145732
  38.0 10.8 %collective-permute-start.6 = (bf16[256,1024]{1,0:T(8,128)(2,1)S(1)}, bf16[256,1024]{1,0:T(8,128)(2,1)S(1)}, u32[]{:S(2)}, u32[]{:S(2)}) collective-permute-start(bf16[256,1024]{1,0:T(8,128)(2,1)S(1)} %shard_map.83), channel_id=1, source_target_pairs={{0,1},{1,0},{2,3},{3,2},{4,5},{5,4},{6,7},{7,6},{8,9},{9,8},{10,11... | collective-permute-start | bytes 1572872 | tf_op jit(solution)/shard_map/ppermute | solution.py:21
  38.8 7.1 %collective-permute-start.8 = (bf16[512,256]{1,0:T(8,128)(2,1)S(1)}, bf16[512,256]{1,0:T(8,128)(2,1)S(1)}, u32[]{:S(2)}, u32[]{:S(2)}) collective-permute-start(bf16[512,256]{1,0:T(8,128)(2,1)S(1)} %copy-done.10), channel_id=1, source_target_pairs={{0,1},{1,0},{2,3},{3,2},{4,5},{5,4},{6,7},{7,6},{8,9},{9,8},{10,11... | collective-permute-start | bytes 786440 | tf_op jit(solution)/shard_map/ppermute | solution.py:21
  38.8 10.0 %collective-permute-start.9 = (bf16[512,256]{1,0:T(8,128)(2,1)}, bf16[512,256]{1,0:T(8,128)(2,1)S(1)}, u32[]{:S(2)}, u32[]{:S(2)}) collective-permute-start(bf16[512,256]{1,0:T(8,128)(2,1)} %collective-permute-done.5.refs_12_), channel_id=1, source_target_pairs={{0,1},{1,0},{2,3},{3,2},{4,5},{5,4},{6,7},{7,6},{8,9},{9,8},{10,11... | collective-permute-start | bytes 786440 | tf_op jit(solution)/shard_map/ppermute | solution.py:21
  39.9 13.2 %collective-permute-start.26 = (bf16[256,512]{1,0:T(8,128)(2,1)}, bf16[256,512]{1,0:T(8,128)(2,1)}, u32[]{:S(2)}, u32[]{:S(2)}) collective-permute-start(bf16[256,512]{1,0:T(8,128)(2,1)} %param.12), channel_id=1, source_target_pairs={{0,1},{1,0},{2,3},{3,2},{4,5},{5,4},{6,7},{7,6},{8,9},{9,8},{10,11... | collective-permute-start | bytes 786440 | tf_op jit(solution)/shard_map/ppermute | solution.py:21
  45.1 3.7 %collective-permute-start.11 = (bf16[256,256]{1,0:T(8,128)(2,1)S(1)}, bf16[256,256]{1,0:T(8,128)(2,1)S(1)}, u32[]{:S(2)}, u32[]{:S(2)}) collective-permute-start(bf16[256,256]{1,0:T(8,128)(2,1)S(1)} %collective-permute-done.10.refs_14_), channel_id=1, source_target_pairs={{0,1},{1,0},{2,3},{3,2},{4,5},{5,4},{6,7},{7,6},{8,9},{9,8},{10,11... | collective-permute-start | bytes 393224 | tf_op jit(solution)/shard_map/ppermute | solution.py:21
  45.9 10.4 %collective-permute-start.19 = (bf16[256,512]{1,0:T(8,128)(2,1)}, bf16[256,512]{1,0:T(8,128)(2,1)}, u32[]{:S(2)}, u32[]{:S(2)}) collective-permute-start(bf16[256,512]{1,0:T(8,128)(2,1)} %constant_dynamic-slice_fusion.1), channel_id=1, source_target_pairs={{0,8},{1,5},{2,10},{3,7},{8,16},{9,1},{10,18},{11,3},{16,24},{17,9... | collective-permute-start | bytes 786440 | tf_op jit(solution)/shard_map/ppermute | solution.py:36
  52.4 5.7 %collective-permute-start.22 = (bf16[256,256]{1,0:T(8,128)(2,1)}, bf16[256,256]{1,0:T(8,128)(2,1)S(1)}, u32[]{:S(2)}, u32[]{:S(2)}) collective-permute-start(bf16[256,256]{1,0:T(8,128)(2,1)} %get-tuple-element.26.near0), channel_id=1, source_target_pairs={{0,4},{4,0},{8,12},{12,8},{16,20},{20,16},{24,28},{28,24},{1,5},{5... | collective-permute-start | bytes 393224 | tf_op jit(solution)/shard_map/ppermute | solution.py:21
  54.4 16.6 %copy-start.3 = (bf16[256,1024]{1,0:T(8,128)(2,1)S(1)}, bf16[256,1024]{1,0:T(8,128)(2,1)}, u32[]{:S(2)}) copy-start(bf16[256,1024]{1,0:T(8,128)(2,1)} %copy-done.2) | copy-start | bytes 1572868
  54.4 16.6 %collective-permute-start.14 = (bf16[512,512]{1,0:T(8,128)(2,1)}, bf16[512,512]{1,0:T(8,128)(2,1)}, u32[]{:S(2)}, u32[]{:S(2)}) collective-permute-start(bf16[512,512]{1,0:T(8,128)(2,1)} %collective-permute-done.13.refs_8_), channel_id=1, source_target_pairs={{0,1},{1,0},{2,3},{3,2},{4,5},{5,4},{6,7},{7,6},{8,9},{9,8},{10,11... | collective-permute-start | bytes 1572872 | tf_op jit(solution)/shard_map/ppermute | solution.py:21
  55.8 15.2 %collective-permute-start.16 = (bf16[512,512]{1,0:T(8,128)(2,1)}, bf16[512,512]{1,0:T(8,128)(2,1)}, u32[]{:S(2)}, u32[]{:S(2)}) collective-permute-start(bf16[512,512]{1,0:T(8,128)(2,1)} %collective-permute-done.15.refs_10_), channel_id=1, source_target_pairs={{0,1},{1,0},{2,3},{3,2},{4,5},{5,4},{6,7},{7,6},{8,9},{9,8},{10,11... | collective-permute-start | bytes 1572872 | tf_op jit(solution)/shard_map/ppermute | solution.py:21
  55.9 15.1 %collective-permute-start.18 = (bf16[512,512]{1,0:T(8,128)(2,1)S(1)}, bf16[512,512]{1,0:T(8,128)(2,1)}, u32[]{:S(2)}, u32[]{:S(2)}) collective-permute-start(bf16[512,512]{1,0:T(8,128)(2,1)S(1)} %copy-done.5), channel_id=1, source_target_pairs={{0,1},{1,0},{2,3},{3,2},{4,5},{5,4},{6,7},{7,6},{8,9},{9,8},{10,11... | collective-permute-start | bytes 1572872 | tf_op jit(solution)/shard_map/ppermute | solution.py:21
  56.4 12.0 %collective-permute-start.27 = (bf16[512,512]{1,0:T(8,128)(2,1)S(1)}, bf16[512,512]{1,0:T(8,128)(2,1)S(1)}, u32[]{:S(2)}, u32[]{:S(2)}) collective-permute-start(bf16[512,512]{1,0:T(8,128)(2,1)S(1)} %maximum_select_fusion.1.refs_0_), channel_id=1, source_target_pairs={{0,8},{1,5},{2,10},{3,7},{8,16},{9,1},{10,18},{11,3},{16,24},{17,9... | collective-permute-start | bytes 1572872 | tf_op jit(solution)/shard_map/ppermute | solution.py:36
  59.0 8.5 %collective-permute-start.23 = (bf16[256,256]{1,0:T(8,128)(2,1)S(1)}, bf16[256,256]{1,0:T(8,128)(2,1)}, u32[]{:S(2)}, u32[]{:S(2)}) collective-permute-start(bf16[256,256]{1,0:T(8,128)(2,1)S(1)} %broadcast_select_fusion), channel_id=1, source_target_pairs={{0,8},{4,12},{8,0},{12,4},{16,24},{20,28},{24,16},{28,20},{1,9},{5... | collective-permute-start | bytes 393224 | tf_op jit(solution)/shard_map/ppermute | solution.py:21
  60.5 10.5 %copy-start.6 = (f32[256,128]{1,0:T(8,128)S(1)}, f32[256,128]{1,0:T(8,128)}, u32[]{:S(2)}) copy-start(f32[256,128]{1,0:T(8,128)} %get-tuple-element.47.refs_1_) | copy-start | bytes 393220
  60.5 10.6 %copy-start.14 = (f32[256,128]{1,0:T(8,128)S(1)}, f32[256,128]{1,0:T(8,128)}, u32[]{:S(2)}) copy-start(f32[256,128]{1,0:T(8,128)} %copy-done.13) | copy-start | bytes 393220
  67.4 3.6 %collective-permute-start.20 = (bf16[256,512]{1,0:T(8,128)(2,1)}, bf16[256,512]{1,0:T(8,128)(2,1)S(1)}, u32[]{:S(2)}, u32[]{:S(2)}) collective-permute-start(bf16[256,512]{1,0:T(8,128)(2,1)} %collective-permute-done.19.refs_14_), channel_id=1, source_target_pairs={{0,1},{1,0},{2,3},{3,2},{4,5},{5,4},{6,7},{7,6},{8,9},{9,8},{10,11... | collective-permute-start | bytes 786440 | tf_op jit(solution)/shard_map/ppermute | solution.py:21
  68.4 16.4 %collective-permute-start.29 = (bf16[512,512]{1,0:T(8,128)(2,1)S(1)}, bf16[512,512]{1,0:T(8,128)(2,1)}, u32[]{:S(2)}, u32[]{:S(2)}) collective-permute-start(bf16[512,512]{1,0:T(8,128)(2,1)S(1)} %collective-permute-done.27.refs_1_), channel_id=1, source_target_pairs={{0,8},{1,5},{2,10},{3,7},{8,16},{9,1},{10,18},{11,3},{16,24},{17,9... | collective-permute-start | bytes 1572872 | tf_op jit(solution)/shard_map/ppermute | solution.py:36
  75.5 9.3 %collective-permute-start.24 = (bf16[256,256]{1,0:T(8,128)(2,1)S(1)}, bf16[256,256]{1,0:T(8,128)(2,1)S(1)}, u32[]{:S(2)}, u32[]{:S(2)}) collective-permute-start(bf16[256,256]{1,0:T(8,128)(2,1)S(1)} %broadcast_select_fusion.1), channel_id=1, source_target_pairs={{0,16},{4,20},{8,24},{12,28},{16,0},{20,4},{24,8},{28,12},{1,17},{... | collective-permute-start | bytes 393224 | tf_op jit(solution)/shard_map/ppermute | solution.py:21
  84.8 9.4 %collective-permute-start.31 = (bf16[512,512]{1,0:T(8,128)(2,1)}, bf16[512,512]{1,0:T(8,128)(2,1)S(1)}, u32[]{:S(2)}, u32[]{:S(2)}) collective-permute-start(bf16[512,512]{1,0:T(8,128)(2,1)} %collective-permute-done.29.refs_0_), channel_id=1, source_target_pairs={{0,8},{1,5},{2,10},{3,7},{8,16},{9,1},{10,18},{11,3},{16,24},{17,9... | collective-permute-start | bytes 1572872 | tf_op jit(solution)/shard_map/ppermute | solution.py:36
  84.9 15.9 %collective-permute-start.28 = (bf16[512,512]{1,0:T(8,128)(2,1)S(1)}, bf16[512,512]{1,0:T(8,128)(2,1)S(1)}, u32[]{:S(2)}, u32[]{:S(2)}) collective-permute-start(bf16[512,512]{1,0:T(8,128)(2,1)S(1)} %collective-permute-done.27.refs_1_), channel_id=1, source_target_pairs={{0,1},{1,0},{2,3},{3,2},{4,5},{5,4},{6,7},{7,6},{8,9},{9,8},{10,11... | collective-permute-start | bytes 1572872 | tf_op jit(solution)/shard_map/ppermute | solution.py:21
  85.0 9.3 %collective-permute-start.21 = (bf16[256,256]{1,0:T(8,128)(2,1)}, bf16[256,256]{1,0:T(8,128)(2,1)S(1)}, u32[]{:S(2)}, u32[]{:S(2)}) collective-permute-start(bf16[256,256]{1,0:T(8,128)(2,1)} %get-tuple-element.26.near0), channel_id=1, source_target_pairs={{0,1},{1,0},{2,3},{3,2},{4,5},{5,4},{6,7},{7,6},{8,9},{9,8},{10,11... | collective-permute-start | bytes 393224 | tf_op jit(solution)/shard_map/ppermute | solution.py:21
  85.5 17.6 %collective-permute-start.30 = (bf16[512,512]{1,0:T(8,128)(2,1)}, bf16[512,512]{1,0:T(8,128)(2,1)S(1)}, u32[]{:S(2)}, u32[]{:S(2)}) collective-permute-start(bf16[512,512]{1,0:T(8,128)(2,1)} %collective-permute-done.29.refs_0_), channel_id=1, source_target_pairs={{0,1},{1,0},{2,3},{3,2},{4,5},{5,4},{6,7},{7,6},{8,9},{9,8},{10,11... | collective-permute-start | bytes 1572872 | tf_op jit(solution)/shard_map/ppermute | solution.py:21
  85.5 8.8 %copy-start.17 = (s32[1,4,4]{2,1,0:T(4,128)S(1)}, s32[1,4,4]{2,1,0:T(4,128)}, u32[]{:S(2)}) copy-start(s32[1,4,4]{2,1,0:T(4,128)} %param.14) | copy-start | bytes 196
  85.6 8.9 %copy-start.12 = (bf16[256,512]{1,0:T(8,128)(2,1)S(1)}, bf16[256,512]{1,0:T(8,128)(2,1)}, u32[]{:S(2)}) copy-start(bf16[256,512]{1,0:T(8,128)(2,1)} %copy-done.11) | copy-start | bytes 786436
  85.6 8.9 %collective-permute-start.25 = (bf16[256,256]{1,0:T(8,128)(2,1)S(1)}, bf16[256,256]{1,0:T(8,128)(2,1)S(1)}, u32[]{:S(2)}, u32[]{:S(2)}) collective-permute-start(bf16[256,256]{1,0:T(8,128)(2,1)S(1)} %broadcast_select_fusion.2.far0), channel_id=1, source_target_pairs={{0,1},{1,0},{2,3},{3,2},{4,5},{5,4},{6,7},{7,6},{8,9},{9,8},{10,11... | collective-permute-start | bytes 393224 | tf_op jit(solution)/shard_map/ppermute | solution.py:21
  94.3 10.9 %collective-permute-start.32 = (bf16[512,512]{1,0:T(8,128)(2,1)S(1)}, bf16[512,512]{1,0:T(8,128)(2,1)S(1)}, u32[]{:S(2)}, u32[]{:S(2)}) collective-permute-start(bf16[512,512]{1,0:T(8,128)(2,1)S(1)} %collective-permute-done.31.refs_0_), channel_id=1, source_target_pairs={{0,1},{1,0},{2,3},{3,2},{4,5},{5,4},{6,7},{7,6},{8,9},{9,8},{10,11... | collective-permute-start | bytes 1572872 | tf_op jit(solution)/shard_map/ppermute | solution.py:21
  94.3 6.4 %collective-permute-start.33 = (bf16[256,512]{1,0:T(8,128)(2,1)S(1)}, bf16[256,512]{1,0:T(8,128)(2,1)S(1)}, u32[]{:S(2)}, u32[]{:S(2)}) collective-permute-start(bf16[256,512]{1,0:T(8,128)(2,1)S(1)} %constant_dynamic-slice_fusion), channel_id=1, source_target_pairs={{0,8},{1,5},{2,10},{3,7},{8,16},{9,1},{10,18},{11,3},{16,24},{17,9... | collective-permute-start | bytes 786440 | tf_op jit(solution)/shard_map/ppermute | solution.py:36
  100.7 6.6 %collective-permute-start.34 = (bf16[256,512]{1,0:T(8,128)(2,1)S(1)}, bf16[256,512]{1,0:T(8,128)(2,1)S(1)}, u32[]{:S(2)}, u32[]{:S(2)}) collective-permute-start(bf16[256,512]{1,0:T(8,128)(2,1)S(1)} %collective-permute-done.33.refs_0_), channel_id=1, source_target_pairs={{0,1},{1,0},{2,3},{3,2},{4,5},{5,4},{6,7},{7,6},{8,9},{9,8},{10,11... | collective-permute-start | bytes 786440 | tf_op jit(solution)/shard_map/ppermute | solution.py:21
  101.5 12.0 %collective-permute-start.35 = (bf16[128,1536]{1,0:T(8,128)(2,1)S(1)}, bf16[128,1536]{1,0:T(8,128)(2,1)S(1)}, u32[]{:S(2)}, u32[]{:S(2)}) collective-permute-start(bf16[128,1536]{1,0:T(8,128)(2,1)S(1)} %get-tuple-element.35), channel_id=1, source_target_pairs={{0,2},{1,3},{2,0},{3,1},{4,6},{5,7},{6,4},{7,5},{8,10},{9,11},{10,... | collective-permute-start | bytes 1179656 | tf_op jit(solution)/shard_map/ppermute | solution.py:21
  104.6 14.5 %collective-permute-start.36 = (bf16[128,1024]{1,0:T(8,128)(2,1)S(1)}, bf16[128,1024]{1,0:T(8,128)(2,1)S(1)}, u32[]{:S(2)}, u32[]{:S(2)}) collective-permute-start(bf16[128,1024]{1,0:T(8,128)(2,1)S(1)} %get-tuple-element.36), channel_id=1, source_target_pairs={{0,2},{1,3},{2,0},{3,1},{4,6},{5,7},{6,4},{7,5},{8,10},{9,11},{10,... | collective-permute-start | bytes 786440 | tf_op jit(solution)/shard_map/ppermute | solution.py:21
  105.7 21.4 %collective-permute-start.37 = (bf16[128,1024]{1,0:T(8,128)(2,1)S(1)}, bf16[128,1024]{1,0:T(8,128)(2,1)S(1)}, u32[]{:S(2)}, u32[]{:S(2)}) collective-permute-start(bf16[128,1024]{1,0:T(8,128)(2,1)S(1)} %get-tuple-element.37), channel_id=1, source_target_pairs={{0,2},{1,3},{2,0},{3,1},{4,6},{5,7},{6,4},{7,5},{8,10},{9,11},{10,... | collective-permute-start | bytes 786440 | tf_op jit(solution)/shard_map/ppermute | solution.py:21
  107.7 19.4 %collective-permute-start.38 = (bf16[128,512]{1,0:T(8,128)(2,1)S(1)}, bf16[128,512]{1,0:T(8,128)(2,1)S(1)}, u32[]{:S(2)}, u32[]{:S(2)}) collective-permute-start(bf16[128,512]{1,0:T(8,128)(2,1)S(1)} %get-tuple-element.38), channel_id=1, source_target_pairs={{0,2},{1,3},{2,0},{3,1},{4,6},{5,7},{6,4},{7,5},{8,10},{9,11},{10,... | collective-permute-start | bytes 393224 | tf_op jit(solution)/shard_map/ppermute | solution.py:21
  (9 other events, 29.5 us)
